TPU v7x, 32 devices: a whole 2x2x4 slice. The times are simulated.
32 devices in a mesh: dp: 8 (over z, y), mp: 4 (over x, core).
Axes of the slice: x: 2, y: 2, z: 4, core: 2. Of those that a mesh axis runs over, the one named last changes fastest.
Arguments:
- tokens: bfloat16 [16384, 1024], P(('dp', 'mp')), may hold values from -6 to 6
- cotangent: bfloat16 [16384, 1024], P(('dp', 'mp')), may hold values from -6 to 6
- item_lengths: int32 [40], P('dp'), may hold values from 0 to 1024, as said below
- gsd_ratio: float32 [40], P('dp'), may hold values from 0.25 to 1
- ln1_gain: bfloat16 [1024], replicated, may hold values from 0.5 to 1.5
- ln1_bias: bfloat16 [1024], replicated, may hold values from -1.1953125 to 1.1953125
- w_qkv: bfloat16 [3, 1024, 1024], P(None, 'mp'), may hold values from -0.1875 to 0.1875
- qv_bias: float32 [2, 1024], P(None, 'mp'), may hold values from -3 to 3
- w_out: bfloat16 [1024, 1024], P('mp'), may hold values from -1.5 to 1.5
- out_bias: float32 [1024], replicated, may hold values from -1.2 to 1.2
- ln2_gain: float32 [1024], replicated, may hold values from 0.5 to 1.5
- ln2_bias: float32 [1024], replicated, may hold values from -1.2 to 1.2
- w_up: bfloat16 [1024, 4096], P(None, 'mp'), may hold values from -0.1875 to 0.1875
- up_bias: float32 [4096], P('mp'), may hold values from -1.8 to 1.8
- w_down: bfloat16 [4096, 1024], P('mp'), may hold values from -0.09375 to 0.09375
- down_bias: float32 [1024], replicated, may hold values from -1.2 to 1.2
Outputs:
- output: bfloat16 [16384, 1024], P(('dp', 'mp'))
- input_grad: float32 [16384, 1024], P(('dp', 'mp'))
- grad_ln1_gain: float32 [1024], replicated
- grad_ln1_bias: float32 [1024], replicated
- grad_qkv: float32 [3, 1024, 1024], P(None, 'mp')
- grad_qv_bias: float32 [2, 1024], P(None, 'mp')
- grad_out_weight: float32 [1024, 1024], P('mp')
- grad_out_bias: float32 [1024], replicated
- grad_ln2_gain: float32 [1024], replicated
- grad_ln2_bias: float32 [1024], replicated
- grad_up: float32 [1024, 4096], P(None, 'mp')
- grad_up_bias: float32 [4096], P('mp')
- grad_down: float32 [4096, 1024], P('mp')
- grad_down_bias: float32 [1024], replicated
- stats: float32 [3], replicated
Inputs may be any that keep to these rules, and one draw needn't show every extreme that they name: `item_lengths`: in each block of 5 entries the first is a scene of 512 to 1024 patches, exactly 1024 in some block of every draw; the others are chips of 64 to 256 patches, nonzero ones first, then zeros; the items of a block fit in its 2048 rows and the rows after them are padding.
All inputs are finite; a program needn't handle non-finite values.
Results may differ from a plain program's by a relative error of at most 0.02.
Values may be sent and summed in bfloat16 or wider, within the bound.
No kernel may reach another device: no remote copies, remote signals or barrier semaphores. Data moves between devices by JAX's collectives and lax.ppermute only.
A program may use at most 192 MiB of HBM per device.

v0:
```python
import math

import jax
import jax.numpy as jnp
from jax import lax
from jax.sharding import PartitionSpec as P

HD = 64


EPS = 1e-06
MASKED = -1e30


def layout(lengths, row_count):
    item_count = lengths.shape[0]
    item_ends = jnp.cumsum(lengths)
    item_starts = item_ends - lengths
    places = jnp.arange(row_count, dtype=jnp.int32)
    segment = jnp.sum((places[:, None] >= item_ends[None, :]).astype(jnp.int32), axis=1)
    picked = segment[:, None] == jnp.arange(item_count, dtype=jnp.int32)[None, :]
    offset = jnp.sum(jnp.where(picked, item_starts[None, :], 0), axis=1)
    position = jnp.where(segment < item_count, places - offset, 0)
    return (segment, position, picked)


def encoding(position, row_ratio, columns, full_width):
    half_width = full_width // 2
    freq_index = jnp.where(columns < half_width, columns, columns - half_width).astype(jnp.float32)
    frequency = jnp.exp(freq_index * (-math.log(10000.0) / half_width))
    angles = (position.astype(jnp.float32) * row_ratio)[:, None] * frequency[None, :]
    return jnp.where((columns < half_width)[None, :], jnp.sin(angles), jnp.cos(angles))


def normalize(stream):
    centred = stream - jnp.mean(stream, axis=1, keepdims=True)
    rstd = lax.rsqrt(jnp.mean(centred * centred, axis=1, keepdims=True) + EPS)
    return (centred * rstd, rstd)


def norm_back(gradient, scaled, gain, rstd):
    spread_grad = gradient * gain
    first_mean = jnp.mean(spread_grad, axis=1, keepdims=True)
    second_mean = jnp.mean(spread_grad * scaled, axis=1, keepdims=True)
    return rstd * (spread_grad - first_mean - scaled * second_mean)


def attend(query_rows, key_rows, value_rows, segment):
    row_count, head_count, head_size = query_rows.shape
    block_rows = min(512, row_count)
    block_count = row_count // block_rows
    score_scale = head_size ** (-0.5)
    query_blocks = query_rows.reshape(block_count, block_rows, head_count, head_size)
    segment_blocks = segment.reshape(block_count, block_rows)

    def block_step(carried, inputs):
        query_part, segment_part = inputs
        scores = (
            jnp.einsum("qhd,khd->hqk", query_part, key_rows, preferred_element_type=jnp.float32)
            * score_scale
        )
        same_item = (segment_part[:, None] == segment[None, :])[None]
        scores = jnp.where(same_item, scores, MASKED)
        row_top = jnp.max(scores, axis=-1, keepdims=True)
        exponent = jnp.exp(scores - row_top)
        row_total = jnp.sum(exponent, axis=-1, keepdims=True)
        probs = (exponent / row_total).astype(jnp.bfloat16)
        attn_mixed = jnp.einsum(
            "hqk,khd->qhd", probs, value_rows, preferred_element_type=jnp.float32
        )
        return (carried, (attn_mixed.astype(jnp.bfloat16), (row_top + jnp.log(row_total))[..., 0]))

    _, (attn_mixed, logsum) = lax.scan(block_step, 0, (query_blocks, segment_blocks))
    return (attn_mixed.reshape(row_count, head_count, head_size), logsum)


def attend_back(query_rows, key_rows, value_rows, segment, logsum, grad_mixed):
    row_count, head_count, head_size = query_rows.shape
    block_rows = min(512, row_count)
    block_count = row_count // block_rows
    score_scale = head_size ** (-0.5)
    query_blocks = query_rows.reshape(block_count, block_rows, head_count, head_size)
    segment_blocks = segment.reshape(block_count, block_rows)
    grad_blocks = grad_mixed.reshape(block_count, block_rows, head_count, head_size)

    def block_step(carried, inputs):
        grad_keys, grad_values = carried
        query_part, segment_part, logsum_part, grad_part = inputs
        scores = (
            jnp.einsum("qhd,khd->hqk", query_part, key_rows, preferred_element_type=jnp.float32)
            * score_scale
        )
        same_item = (segment_part[:, None] == segment[None, :])[None]
        probs = jnp.where(same_item, jnp.exp(scores - logsum_part[..., None]), 0.0)
        grad_values = grad_values + jnp.einsum(
            "hqk,qhd->khd",
            probs.astype(jnp.bfloat16),
            grad_part,
            preferred_element_type=jnp.float32,
        )
        grad_probs = jnp.einsum(
            "qhd,khd->hqk", grad_part, value_rows, preferred_element_type=jnp.float32
        )
        centre = jnp.sum(probs * grad_probs, axis=-1, keepdims=True)
        grad_scores = (probs * (grad_probs - centre)).astype(jnp.bfloat16)
        grad_query = (
            jnp.einsum("hqk,khd->qhd", grad_scores, key_rows, preferred_element_type=jnp.float32)
            * score_scale
        )
        grad_keys = (
            grad_keys
            + jnp.einsum(
                "hqk,qhd->khd", grad_scores, query_part, preferred_element_type=jnp.float32
            )
            * score_scale
        )
        return ((grad_keys, grad_values), grad_query.astype(jnp.bfloat16))

    zero_grads = jnp.zeros(key_rows.shape, jnp.float32)
    (grad_keys, grad_values), grad_query = lax.scan(
        block_step, (zero_grads, zero_grads), (query_blocks, segment_blocks, logsum, grad_blocks)
    )
    return (
        grad_query.reshape(row_count, head_count, head_size),
        grad_keys.astype(jnp.bfloat16),
        grad_values.astype(jnp.bfloat16),
    )


def per_device(
    tokens,
    cotangent,
    item_lengths,
    gsd_ratio,
    ln1_gain,
    ln1_bias,
    w_qkv,
    qv_bias,
    w_out,
    out_bias,
    ln2_gain,
    ln2_bias,
    w_up,
    up_bias,
    w_down,
    down_bias,
):
    own_count, full_width = tokens.shape
    mp_count = lax.axis_size("mp")
    row_count = own_count * mp_count
    first_row = lax.axis_index("mp") * own_count
    item_count = item_lengths.shape[0]
    segment, position, picked = layout(item_lengths, row_count)
    valid_rows = (segment < item_count).astype(jnp.float32)[:, None]
    row_ratio = jnp.sum(jnp.where(picked, gsd_ratio[None, :], 0.0), axis=1)

    def own(array):
        return lax.dynamic_slice_in_dim(array, first_row, own_count, 0)

    valid_own = own(valid_rows)
    gathered = lax.all_gather(tokens, "mp", axis=0, tiled=True)
    columns = jnp.arange(full_width, dtype=jnp.int32)
    stream0 = gathered.astype(jnp.float32) + encoding(position, row_ratio, columns, full_width)
    scaled1, rstd_all = normalize(stream0)
    normed1 = (scaled1 * ln1_gain.astype(jnp.float32) + ln1_bias.astype(jnp.float32)).astype(
        jnp.bfloat16
    )
    mine_first = own(scaled1)
    rstd_first = own(rstd_all)
    head_count = w_qkv.shape[1] // HD
    projected = jnp.einsum("rd,ced->cre", normed1, w_qkv, preferred_element_type=jnp.float32)
    query_rows = (projected[0] + qv_bias[0]).astype(jnp.bfloat16).reshape(row_count, head_count, HD)
    key_rows = projected[1].astype(jnp.bfloat16).reshape(row_count, head_count, HD)
    value_rows = (projected[2] + qv_bias[1]).astype(jnp.bfloat16).reshape(row_count, head_count, HD)
    attn_mixed, logsum = attend(query_rows, key_rows, value_rows, segment)
    attended = attn_mixed.reshape(row_count, head_count * HD)
    attn_part = jnp.dot(attended, w_out, preferred_element_type=jnp.float32)
    attn_full = lax.psum(attn_part.astype(jnp.bfloat16), "mp").astype(jnp.float32) + out_bias
    stream1 = stream0 + attn_full
    scaled2, rstd_full = normalize(stream1)
    normed2 = (scaled2 * ln2_gain + ln2_bias).astype(jnp.bfloat16)
    attn_mine = own(attn_full)
    stream1_mine = own(stream1)
    mine_second = own(scaled2)
    rstd_second = own(rstd_full)
    up_value = jnp.dot(normed2, w_up, preferred_element_type=jnp.float32) + up_bias
    activation = jax.nn.gelu(up_value, approximate=False).astype(jnp.bfloat16)
    mlp_part = jnp.dot(activation, w_down, preferred_element_type=jnp.float32)
    mlp_mine = (
        lax.psum_scatter(
            mlp_part.astype(jnp.bfloat16), "mp", scatter_dimension=0, tiled=True
        ).astype(jnp.float32)
        + down_bias
    )
    stream2 = stream1_mine + mlp_mine
    output = (valid_own * stream2).astype(jnp.bfloat16)
    square_sums = jnp.stack(
        [
            jnp.sum(valid_own * stream2 * stream2),
            jnp.sum(valid_own * attn_mine * attn_mine),
            jnp.sum(valid_own * mlp_mine * mlp_mine),
            jnp.sum(valid_own),
        ]
    )

    def full_rows(gradient):
        return lax.all_gather(gradient, "mp", axis=0, tiled=True)

    def own_rows(partial_sum):
        return lax.psum_scatter(
            partial_sum.astype(jnp.bfloat16), "mp", scatter_dimension=0, tiled=True
        ).astype(jnp.float32)

    grad_stream2 = valid_own * cotangent.astype(jnp.float32)
    grad_mlp = grad_stream2.astype(jnp.bfloat16)
    grad_down_bias = jnp.sum(grad_mlp.astype(jnp.float32), axis=0)
    mlp_rows = full_rows(grad_mlp)
    grad_down = jnp.einsum("rf,rd->fd", activation, mlp_rows, preferred_element_type=jnp.float32)
    grad_act = jnp.einsum("rd,fd->rf", mlp_rows, w_down, preferred_element_type=jnp.float32)
    _, gelu_back = jax.vjp(lambda inputs: jax.nn.gelu(inputs, approximate=False), up_value)
    grad_upin = gelu_back(grad_act)[0].astype(jnp.bfloat16)
    grad_up = jnp.einsum("rd,rf->df", normed2, grad_upin, preferred_element_type=jnp.float32)
    grad_up_bias = jnp.sum(grad_upin.astype(jnp.float32), axis=0)
    grad_norm2 = own_rows(
        jnp.einsum("rf,df->rd", grad_upin, w_up, preferred_element_type=jnp.float32)
    )
    grad_ln2_gain = jnp.sum(grad_norm2 * mine_second, axis=0)
    grad_ln2_bias = jnp.sum(grad_norm2, axis=0)
    grad_stream1 = grad_stream2 + norm_back(grad_norm2, mine_second, ln2_gain, rstd_second)
    grad_attn = grad_stream1.astype(jnp.bfloat16)
    grad_out_bias = jnp.sum(grad_attn.astype(jnp.float32), axis=0)
    attn_rows = full_rows(grad_attn)
    grad_out_weight = jnp.einsum(
        "rc,rd->cd", attended, attn_rows, preferred_element_type=jnp.float32
    )
    grad_attended = jnp.einsum(
        "rd,cd->rc", attn_rows, w_out, preferred_element_type=jnp.float32
    ).astype(jnp.bfloat16)
    grad_query, grad_keys, grad_values = attend_back(
        query_rows,
        key_rows,
        value_rows,
        segment,
        logsum,
        grad_attended.reshape(row_count, head_count, HD),
    )
    grad_proj = jnp.stack(
        [
            grad_query.reshape(row_count, head_count * HD),
            grad_keys.reshape(row_count, head_count * HD),
            grad_values.reshape(row_count, head_count * HD),
        ]
    )
    grad_qkv = jnp.einsum("cre,rd->ced", grad_proj, normed1, preferred_element_type=jnp.float32)
    grad_qv_bias = jnp.stack(
        [
            jnp.sum(grad_proj[0].astype(jnp.float32), axis=0),
            jnp.sum(grad_proj[2].astype(jnp.float32), axis=0),
        ]
    )
    grad_norm1 = own_rows(
        jnp.einsum("cre,ced->rd", grad_proj, w_qkv, preferred_element_type=jnp.float32)
    )
    grad_ln1_gain = jnp.sum(grad_norm1 * mine_first, axis=0)
    grad_ln1_bias = jnp.sum(grad_norm1, axis=0)
    input_grad = grad_stream1 + norm_back(
        grad_norm1, mine_first, ln1_gain.astype(jnp.float32), rstd_first
    )
    grad_qkv, grad_qv_bias, grad_out_weight, grad_up, grad_up_bias, grad_down = (
        lax.psum(grad_qkv.astype(jnp.bfloat16), "dp").astype(jnp.float32),
        lax.psum(grad_qv_bias.astype(jnp.bfloat16), "dp").astype(jnp.float32),
        lax.psum(grad_out_weight.astype(jnp.bfloat16), "dp").astype(jnp.float32),
        lax.psum(grad_up.astype(jnp.bfloat16), "dp").astype(jnp.float32),
        lax.psum(grad_up_bias.astype(jnp.bfloat16), "dp").astype(jnp.float32),
        lax.psum(grad_down.astype(jnp.bfloat16), "dp").astype(jnp.float32),
    )
    (
        summed_squares,
        grad_ln1_gain,
        grad_ln1_bias,
        grad_out_bias,
        grad_ln2_gain,
        grad_ln2_bias,
        grad_down_bias,
    ) = lax.psum(
        (
            square_sums,
            grad_ln1_gain,
            grad_ln1_bias,
            grad_out_bias,
            grad_ln2_gain,
            grad_ln2_bias,
            grad_down_bias,
        ),
        ("dp", "mp"),
    )
    stats = jnp.sqrt(summed_squares[:3] / (summed_squares[3] * full_width))
    return (
        output,
        input_grad,
        grad_ln1_gain,
        grad_ln1_bias,
        grad_qkv,
        grad_qv_bias,
        grad_out_weight,
        grad_out_bias,
        grad_ln2_gain,
        grad_ln2_bias,
        grad_up,
        grad_up_bias,
        grad_down,
        grad_down_bias,
        stats,
    )


def solution(mesh):
    placed = (
        P(("dp", "mp"), None),
        P(("dp", "mp"), None),
        P("dp"),
        P("dp"),
        P(),
        P(),
        P(None, "mp", None),
        P(None, "mp"),
        P("mp", None),
        P(),
        P(),
        P(),
        P(None, "mp"),
        P("mp"),
        P("mp", None),
        P(),
    )
    return jax.shard_map(
        per_device,
        mesh=mesh,
        in_specs=placed,
        out_specs=(
            P(("dp", "mp"), None),
            P(("dp", "mp"), None),
            P(),
            P(),
            P(None, "mp", None),
            P(None, "mp"),
            P("mp", None),
            P(),
            P(),
            P(),
            P(None, "mp"),
            P("mp"),
            P("mp", None),
            P(),
            P(),
        ),
        check_vma=False,
    )
```

profile of v0, /device:TPU:0, one launch (start us, length us, event | category | flops | bytes accessed | tf_op | source)
XLA Modules:
  0.0 1076.3 jit_solution(11386181997377346976)
XLA Ops:
  13.4 33.4 %all-gather.4.cloned.1.call-done = bf16[2048,1024]{1,0:T(8,128)(2,1)} async-done(((bf16[512,1024]{1,0:T(8,128)(2,1)}), bf16[2048,1024]{1,0:T(8,128)(2,1)}) %all-gather.4.cloned.1.call-update) | async-done | bytes 4194320 | tf_op jit(solution)/shard_map/all_gather | solution.py:161
  46.8 33.8 %fusion.52 = f32[2048]{0:T(1024)S(1)} fusion(bf16[2048,1024]{1,0:T(8,128)(2,1)} %all-gather.4.cloned.1.call-done, f32[1024]{0:T(1024)S(1)} %fusion.81, f32[2048]{0:T(1024)S(1)} %get-tuple-element.267, pred[1024]{0:T(1024)(128)(4,1)S(1)} %iota_compare_fusion.2), kind=kLoop, calls=%fused_computation.82 | loop fusion | flops 10483712 | bytes 4215808 | tf_op jit(solution)/shard_map/reduce_sum | solution.py:36
  80.6 34.7 %multiply_reduce_fusion.2 = f32[2048]{0:T(1024)S(1)} fusion(bf16[2048,1024]{1,0:T(8,128)(2,1)} %all-gather.4.cloned.1.call-done, f32[2048]{0:T(1024)S(1)} %broadcast_multiply_fusion.1, f32[1024]{0:T(1024)S(1)} %fusion.81, f32[2048]{0:T(1024)S(1)} %get-tuple-element.267, pred[1024]{0:T(1024)(128)(4,1)S(1)} %iota_compare_fusion.2), kind=kLoop, calls=%fused_computation.77 | loop fusion | flops 14678016 | bytes 4224000 | tf_op jit(solution)/shard_map/reduce_sum | solution.py:37
  115.3 31.9 %subtract_multiply_fusion.1 = f32[2048,1024]{1,0:T(8,128)S(1)} fusion(bf16[2048,1024]{1,0:T(8,128)(2,1)S(1)} %copy-done.8, f32[2048]{0:T(1024)S(1)} %add_rsqrt_fusion.1, f32[2048]{0:T(1024)S(1)} %broadcast_multiply_fusion.1, f32[1024]{0:T(1024)S(1)} %fusion.81, f32[2048]{0:T(1024)S(1)} %get-tuple-element.267, pred[1024]{0:T(1024)(128)(4,1)S(1)} %iota_compare_fusion.2), kind=kLoop, calls=%fused_computation.80 | loop fusion | flops 12582912 | bytes 12612608 | tf_op jit(solution)/shard_map/mul | solution.py:38
  164.4 64.1 %while.27 = (s32[]{:T(128)}, bf16[4,512,4,64]{1,3,2,0:T(8,128)(2,1)}, f32[4,4,512]{2,1,0:T(4,128)}, s32[4,512]{1,0:T(4,128)S(1)}, s32[2048]{0:T(1024)S(1)}, /*in...) while((s32[]{:T(128)}, ...), condition=%wide.region_9.10_spmd, body=%wide.region_6.9_spmd.sunk | while | flops 1125251072 | bytes 61421712 | solution.py:73
  173.8 5.9 fusion.140
  189.8 5.9 fusion.140
  205.9 5.9 fusion.140
  221.9 5.9 fusion.140
  240.5 81.7 %all-reduce.6.cloned.1.call-done = bf16[2048,1024]{1,0:T(8,128)(2,1)} async-done(((bf16[2048,1024]{1,0:T(8,128)(2,1)}), bf16[2048,1024]{1,0:T(8,128)(2,1)}) %all-reduce.6.cloned.1.call-update) | async-done | bytes 4194320 | tf_op jit(solution)/shard_map/psum | solution.py:178
  322.2 36.9 %fusion.90 = (f32[2048]{0:T(1024)S(1)}, f32[2048,1024]{1,0:T(8,128)S(1)}, f32[2048,1024]{1,0:T(8,128)}) fusion(f32[1024]{0:T(1024)S(1)} %copy-done.36, bf16[2048,1024]{1,0:T(8,128)(2,1)} %all-reduce.6.cloned.1.call-done, f32[1024]{0:T(1024)S(1)} %copy-done.27, f32[2048]{0:T(1024)S(1)} %copy-done.22, pred[1024]{0:T(1024)(128)(4,1)S(1)} %copy-done.39, ...), kind=kLoop, calls=%fused_computation.166 | loop fusion | flops 16775168 | bytes 25191424 | tf_op jit(solution)/shard_map/reduce_sum | solution.py:36
  366.4 6.7 fusion.76
  373.2 27.5 %fusion.85 = (bf16[1024]{0:T(1024)(128)(2,1)}, bf16[2048,1024]{1,0:T(8,128)(2,1)S(1)}, f32[2048,1024]{1,0:T(8,128)}) fusion(f32[2048,1024]{1,0:T(8,128)} %fusion.76, f32[1024]{0:T(1024)S(1)} %copy-done.37, bf16[2048,1024]{1,0:T(8,128)(2,1)} %all-gather.6.cloned.1.call-done, bf16[1024,1024]{1,0:T(8,128)(2,1)S(1)} %copy-done), kind=kOutput, calls=%fused_computation.164 | convolution fusion | flops 4450155520 | bytes 27269120 | tf_op jit(solution)/shard_map/rd,fd->rf/dot_general | solution.py:219
  402.6 6.3 convolution_convert_fusion.1
  409.5 10.7 multiply_convert_fusion.1
  420.2 8.4 convolution_convert_fusion.2
  428.7 25.1 %reduce-scatter.6.cloned.1.call-done = bf16[512,1024]{1,0:T(8,128)(2,1)} async-done(((bf16[2048,1024]{1,0:T(8,128)(2,1)}), bf16[512,1024]{1,0:T(8,128)(2,1)}) %reduce-scatter.6.cloned.1.call-update) | async-done | bytes 1048592 | tf_op jit(solution)/shard_map/reduce_scatter | solution.py:210
  457.0 44.3 %reduce-scatter.4.cloned.1.call-done = bf16[512,1024]{1,0:T(8,128)(2,1)} async-done(((bf16[2048,1024]{1,0:T(8,128)(2,1)}), bf16[512,1024]{1,0:T(8,128)(2,1)}) %reduce-scatter.4.cloned.1.call-update) | async-done | bytes 1048592 | tf_op jit(solution)/shard_map/reduce_scatter | solution.py:190
  501.3 6.0 fusion.68
  507.3 9.5 convolution_convert_fusion.4
  516.8 9.2 convolution_convert_fusion.5
  526.1 15.8 %all-gather.8.cloned.1.call-done = bf16[2048,1024]{1,0:T(8,128)(2,1)} async-done(((bf16[512,1024]{1,0:T(8,128)(2,1)}), bf16[2048,1024]{1,0:T(8,128)(2,1)}) %all-gather.8.cloned.1.call-update) | async-done | bytes 4194320 | tf_op jit(solution)/shard_map/all_gather | solution.py:207
  549.7 188.2 %while.28 = (s32[]{:T(128)}, f32[2048,4,64]{0,2,1:T(8,128)}, f32[2048,4,64]{0,2,1:T(8,128)}, bf16[4,512,4,64]{1,3,2,0:T(8,128)(2,1)}, bf16[4,512,4,64]{1,3,2,0:T...) while((s32[]{:T(128)}, f32[2048,4,64]{0,2,1:T(8,128)}, ...), condition=%wide.region_19.20_spmd.clone, body=%wide.region_17.19_spmd.clone.sunk | while | flops 2751199232 | bytes 176527568 | solution.py:120
  555.6 6.8 fusion.152
  562.4 11.5 %multiply_reduce_fusion.4 = (f32[4,512]{1,0:T(4,128)}, f32[4,512,2048]{2,1,0:T(8,128)}) fusion(f32[4,512,2048]{2,1,0:T(8,128)S(1)} %fusion.150, f32[4,512]{1,0:T(4,128)} %copy-done.16, pred[512,2048]{1,0:T(8,128)(4,1)S(1)} %broadcast_compare_fusion.7, bf16[2048,4,64]{0,2,1:T(8,128)(2,1)} %get-tuple-element.469, ...), kind=kOutput, calls=%fused_computation.19.clone.1 | convolution fusion | flops 557840384 | bytes 35930116 | tf_op jit(solution)/shard_map/while/body/eval_jaxpr/qhd,khd->hqk/dot_general | solution.py:101
  573.9 11.0 %multiply_convert_fusion.4 = bf16[4,512,2048]{2,1,0:T(8,128)(2,1)} fusion(f32[4,512,2048]{2,1,0:T(8,128)} %get-tuple-element.404, f32[4,512,2048]{2,1,0:T(8,128)S(1)} %fusion.150, f32[4,512]{1,0:T(4,128)} %get-tuple-element.405, f32[4,512]{1,0:T(4,128)} %copy-done.16, pred[512,2048]{1,0:T(8,128)(4,1)S(1)} %broadcast_compare_fusion.7), kind=kLoop, calls=%fused_computation.18.clone.1 | loop fusion | flops 25165824 | bytes 43008000 | tf_op jit(solution)/shard_map/while/body/eval_jaxpr/convert_element_type | solution.py:105
  584.9 7.1 fusion.153
  601.7 7.2 fusion.152
  608.9 11.5 %multiply_reduce_fusion.4 = (f32[4,512]{1,0:T(4,128)}, f32[4,512,2048]{2,1,0:T(8,128)}) fusion(f32[4,512,2048]{2,1,0:T(8,128)S(1)} %fusion.150, f32[4,512]{1,0:T(4,128)} %copy-done.16, pred[512,2048]{1,0:T(8,128)(4,1)S(1)} %broadcast_compare_fusion.7, bf16[2048,4,64]{0,2,1:T(8,128)(2,1)} %get-tuple-element.469, ...), kind=kOutput, calls=%fused_computation.19.clone.1 | convolution fusion | flops 557840384 | bytes 35930116 | tf_op jit(solution)/shard_map/while/body/eval_jaxpr/qhd,khd->hqk/dot_general | solution.py:101
  620.4 11.0 %multiply_convert_fusion.4 = bf16[4,512,2048]{2,1,0:T(8,128)(2,1)} fusion(f32[4,512,2048]{2,1,0:T(8,128)} %get-tuple-element.404, f32[4,512,2048]{2,1,0:T(8,128)S(1)} %fusion.150, f32[4,512]{1,0:T(4,128)} %get-tuple-element.405, f32[4,512]{1,0:T(4,128)} %copy-done.16, pred[512,2048]{1,0:T(8,128)(4,1)S(1)} %broadcast_compare_fusion.7), kind=kLoop, calls=%fused_computation.18.clone.1 | loop fusion | flops 25165824 | bytes 43008000 | tf_op jit(solution)/shard_map/while/body/eval_jaxpr/convert_element_type | solution.py:105
  631.4 7.1 fusion.153
  638.5 4.6 fusion.151
  648.9 7.2 fusion.152
  656.2 11.5 %multiply_reduce_fusion.4 = (f32[4,512]{1,0:T(4,128)}, f32[4,512,2048]{2,1,0:T(8,128)}) fusion(f32[4,512,2048]{2,1,0:T(8,128)S(1)} %fusion.150, f32[4,512]{1,0:T(4,128)} %copy-done.16, pred[512,2048]{1,0:T(8,128)(4,1)S(1)} %broadcast_compare_fusion.7, bf16[2048,4,64]{0,2,1:T(8,128)(2,1)} %get-tuple-element.469, ...), kind=kOutput, calls=%fused_computation.19.clone.1 | convolution fusion | flops 557840384 | bytes 35930116 | tf_op jit(solution)/shard_map/while/body/eval_jaxpr/qhd,khd->hqk/dot_general | solution.py:101
  667.6 11.0 %multiply_convert_fusion.4 = bf16[4,512,2048]{2,1,0:T(8,128)(2,1)} fusion(f32[4,512,2048]{2,1,0:T(8,128)} %get-tuple-element.404, f32[4,512,2048]{2,1,0:T(8,128)S(1)} %fusion.150, f32[4,512]{1,0:T(4,128)} %get-tuple-element.405, f32[4,512]{1,0:T(4,128)} %copy-done.16, pred[512,2048]{1,0:T(8,128)(4,1)S(1)} %broadcast_compare_fusion.7), kind=kLoop, calls=%fused_computation.18.clone.1 | loop fusion | flops 25165824 | bytes 43008000 | tf_op jit(solution)/shard_map/while/body/eval_jaxpr/convert_element_type | solution.py:105
  678.7 7.1 fusion.153
  685.8 4.6 fusion.151
  696.2 7.2 fusion.152
  703.4 11.5 %multiply_reduce_fusion.4 = (f32[4,512]{1,0:T(4,128)}, f32[4,512,2048]{2,1,0:T(8,128)}) fusion(f32[4,512,2048]{2,1,0:T(8,128)S(1)} %fusion.150, f32[4,512]{1,0:T(4,128)} %copy-done.16, pred[512,2048]{1,0:T(8,128)(4,1)S(1)} %broadcast_compare_fusion.7, bf16[2048,4,64]{0,2,1:T(8,128)(2,1)} %get-tuple-element.469, ...), kind=kOutput, calls=%fused_computation.19.clone.1 | convolution fusion | flops 557840384 | bytes 35930116 | tf_op jit(solution)/shard_map/while/body/eval_jaxpr/qhd,khd->hqk/dot_general | solution.py:101
  714.9 11.0 %multiply_convert_fusion.4 = bf16[4,512,2048]{2,1,0:T(8,128)(2,1)} fusion(f32[4,512,2048]{2,1,0:T(8,128)} %get-tuple-element.404, f32[4,512,2048]{2,1,0:T(8,128)S(1)} %fusion.150, f32[4,512]{1,0:T(4,128)} %get-tuple-element.405, f32[4,512]{1,0:T(4,128)} %copy-done.16, pred[512,2048]{1,0:T(8,128)(4,1)S(1)} %broadcast_compare_fusion.7), kind=kLoop, calls=%fused_computation.18.clone.1 | loop fusion | flops 25165824 | bytes 43008000 | tf_op jit(solution)/shard_map/while/body/eval_jaxpr/convert_element_type | solution.py:105
  725.9 7.1 fusion.153
  748.5 8.5 convolution_convert_fusion.6
  759.2 7.2 bitcast_convert_fusion
  771.5 22.6 %all-reduce.1 = (bf16[2,256]{1,0:T(2,128)(2,1)S(1)}, bf16[1024]{0:T(1024)(128)(2,1)S(1)}) all-reduce(bf16[2,256]{1,0:T(2,128)(2,1)S(1)} %pad_maximum_fusion.3, bf16[1024]{0:T(1024)(128)(2,1)S(1)} %copy-done.40), channel_id=1, replica_groups=mesh['dp'=8,'mp'=4] {'dp'}, use_global_device_ids=true, to_apply=%region_30.31 | all-reduce | flops 1536 | bytes 6144 | tf_op jit(solution)/shard_map/psum | solution.py:271
  795.3 179.0 %all-reduce.8.cloned.1.call-done = (bf16[3,256,1024]{2,1,0:T(8,128)(2,1)}, bf16[256,1024]{1,0:T(8,128)(2,1)}, bf16[1024,1024]{1,0:T(8,128)(2,1)}, bf16[1024,1024]{1,0:T(8,128)(2,1)}) async-done(((bf16[3,256,1024]{2,1,0:T(8,128)(2,1)}, bf16[256,1024]{1,0:T(8,128)(2,1)}, bf16[1024,1024]{1,0:T(8,128)(2,1)}, bf16[1024,1024]{1,0:T(8,128)(2,1)}), (bf16[3,256,1024]{2,1,0:T(8,128)(2,1)}, ...) | async-done | bytes 6291472 | tf_op jit(solution)/shard_map/psum | solution.py:270
  980.0 5.1 convert_element_type.206
  987.6 32.6 %reduce-scatter.8.cloned.1.call-done = bf16[512,1024]{1,0:T(8,128)(2,1)} async-done(((bf16[2048,1024]{1,0:T(8,128)(2,1)}), bf16[512,1024]{1,0:T(8,128)(2,1)}) %reduce-scatter.8.cloned.1.call-update) | async-done | bytes 1048592 | tf_op jit(solution)/shard_map/reduce_scatter | solution.py:210
  1023.0 40.1 %all-reduce = (f32[1024]{0:T(1024)}, f32[1024]{0:T(1024)}, f32[1024]{0:T(1024)}, f32[1024]{0:T(1024)}, f32[1024]{0:T(1024)}, /*index=5*/f32[1024]{0:T(1024)}, f32[4]{0:T(128)S(1)}) all-reduce(f32[1024]{0:T(1024)S(1)} %get-tuple-element.193, f32[1024]{0:T(1024)S(1)} %get-tuple-element.200, ...), channel_id=1, replica_groups=mesh['dp'=8,'mp'=4] {'dp','mp'}, use_global_device_ids=true, to_apply=%region_24.25 | all-reduce | flops 6148 | bytes 49184 | tf_op jit(solution)/shard_map/psum | solution.py:285
  (236 shorter events, 163.2 us)
Async XLA Ops:
  7.2 366.0 %copy-start = (bf16[1024,1024]{1,0:T(8,128)(2,1)S(1)}, bf16[1024,1024]{1,0:T(8,128)(2,1)}, u32[]{:S(2)}) copy-start(bf16[1024,1024]{1,0:T(8,128)(2,1)} %param.34) | copy-start | bytes 6291460
  7.2 39.6 %all-gather.4.cloned.1.call-start = ((), (), s32[]{:S(2)}) async-start(), calls=%async_computation.3 | async-start | bytes 5242880 | tf_op jit(solution)/shard_map/all_gather | solution.py:161
  7.9 314.2 %all-reduce.6.cloned.1.call-start = ((), (), s32[]{:S(2)}) async-start(), calls=%async_computation.4 | async-start | bytes 8388608 | tf_op jit(solution)/shard_map/psum | solution.py:178
  10.4 136.8 %copy-start.24 = (f32[1024]{0:T(1024)}, f32[1024]{0:T(1024)S(1)}, u32[]{:S(2)}) copy-start(f32[1024]{0:T(1024)S(1)} %convert_element_type.173) | copy-start | bytes 12292
  11.1 136.1 %copy-start.34 = (f32[1024]{0:T(1024)}, f32[1024]{0:T(1024)S(1)}, u32[]{:S(2)}) copy-start(f32[1024]{0:T(1024)S(1)} %convert_element_type.174) | copy-start | bytes 12292
  11.3 136.0 %copy-start.38 = (pred[1024]{0:T(1024)(128)(4,1)}, pred[1024]{0:T(1024)(128)(4,1)S(1)}, u32[]{:S(2)}) copy-start(pred[1024]{0:T(1024)(128)(4,1)S(1)} %iota_compare_fusion.2) | copy-start | bytes 3076
  11.3 136.0 %copy-start.26 = (f32[1024]{0:T(1024)}, f32[1024]{0:T(1024)S(1)}, u32[]{:S(2)}) copy-start(f32[1024]{0:T(1024)S(1)} %fusion.81) | copy-start | bytes 12292
  13.4 133.9 %copy-start.21 = (f32[2048]{0:T(1024)}, f32[2048]{0:T(1024)S(1)}, u32[]{:S(2)}) copy-start(f32[2048]{0:T(1024)S(1)} %get-tuple-element.267) | copy-start | bytes 24580
  46.8 68.5 %copy-start.8 = (bf16[2048,1024]{1,0:T(8,128)(2,1)S(1)}, bf16[2048,1024]{1,0:T(8,128)(2,1)}, u32[]{:S(2)}) copy-start(bf16[2048,1024]{1,0:T(8,128)(2,1)} %all-gather.4.cloned.1.call-done) | copy-start | bytes 12582916
  80.6 66.7 %copy-start.44 = (bf16[3,256,1024]{2,1,0:T(8,128)(2,1)S(1)}, bf16[3,256,1024]{2,1,0:T(8,128)(2,1)}, u32[]{:S(2)}) copy-start(bf16[3,256,1024]{2,1,0:T(8,128)(2,1)} %param.26) | copy-start | bytes 4718596
  115.3 32.0 %copy-start.23 = (f32[2048]{0:T(1024)}, f32[2048]{0:T(1024)S(1)}, u32[]{:S(2)}) copy-start(f32[2048]{0:T(1024)S(1)} %add_rsqrt_fusion.1) | copy-start | bytes 24580
  228.4 8.1 copy-start.14
  228.4 8.1 copy-start.20
  228.4 131.8 %copy-start.3 = (bf16[2048,4,64]{0,2,1:T(8,128)(2,1)}, bf16[2048,4,64]{0,2,1:T(8,128)(2,1)S(1)}, u32[]{:S(2)}) copy-start(bf16[2048,4,64]{0,2,1:T(8,128)(2,1)S(1)} %get-tuple-element.487) | copy-start | bytes 3145732
  231.1 91.0 %copy-start.22 = (f32[2048]{0:T(1024)S(1)}, f32[2048]{0:T(1024)}, u32[]{:S(2)}) copy-start(f32[2048]{0:T(1024)} %copy-done.21) | copy-start | bytes 24580
  231.2 91.0 %copy-start.27 = (f32[1024]{0:T(1024)S(1)}, f32[1024]{0:T(1024)}, u32[]{:S(2)}) copy-start(f32[1024]{0:T(1024)} %copy-done.26) | copy-start | bytes 12292
  231.2 91.0 %copy-start.36 = (f32[1024]{0:T(1024)S(1)}, f32[1024]{0:T(1024)}, u32[]{:S(2)}) copy-start(f32[1024]{0:T(1024)} %param.29) | copy-start | bytes 12292
  231.2 91.0 %copy-start.39 = (pred[1024]{0:T(1024)(128)(4,1)S(1)}, pred[1024]{0:T(1024)(128)(4,1)}, u32[]{:S(2)}) copy-start(pred[1024]{0:T(1024)(128)(4,1)} %copy-done.38) | copy-start | bytes 3076
  236.6 136.6 %all-gather.6.cloned.1.call-start = ((), (), s32[]{:S(2)}) async-start(), calls=%async_computation.6 | async-start | bytes 5242880 | tf_op jit(solution)/shard_map/all_gather | solution.py:207
  240.5 213.3 %reduce-scatter.6.cloned.1.call-start = ((), (), s32[]{:S(2)}) async-start(), calls=%async_computation.7 | async-start | bytes 5242880 | tf_op jit(solution)/shard_map/reduce_scatter | solution.py:210
  366.4 6.7 copy-start.37
  373.2 29.5 %copy-start.43 = (bf16[1024,1024]{1,0:T(8,128)(2,1)S(1)}, bf16[1024,1024]{1,0:T(8,128)(2,1)}, u32[]{:S(2)}) copy-start(bf16[1024,1024]{1,0:T(8,128)(2,1)} %param.32) | copy-start | bytes 6291460
  408.9 92.3 %reduce-scatter.4.cloned.1.call-start = ((), (), s32[]{:S(2)}) async-start(), calls=%async_computation.5 | async-start | bytes 5242880 | tf_op jit(solution)/shard_map/reduce_scatter | solution.py:190
  420.2 81.1 %copy-start.12 = (bf16[512,1024]{1,0:T(8,128)(2,1)S(1)}, bf16[512,1024]{1,0:T(8,128)(2,1)}, u32[]{:S(2)}) copy-start(bf16[512,1024]{1,0:T(8,128)(2,1)} %param.21) | copy-start | bytes 3145732
  420.2 81.1 %copy-start.33 = (f32[1024]{0:T(1024)S(1)}, f32[1024]{0:T(1024)}, u32[]{:S(2)}) copy-start(f32[1024]{0:T(1024)} %param.35) | copy-start | bytes 12292
  428.5 113.4 %all-gather.8.cloned.1.call-start = ((), (), s32[]{:S(2)}) async-start(), calls=%async_computation.8 | async-start | bytes 5242880 | tf_op jit(solution)/shard_map/all_gather | solution.py:207
  507.3 467.0 %all-reduce.8.cloned.1.call-start = ((), (), s32[]{:S(2)}) async-start(), calls=%async_computation.10 | async-start | bytes 12582912 | tf_op jit(solution)/shard_map/psum | solution.py:270
  507.3 9.5 copy-start.47
  516.8 25.1 %copy-start.19 = (bf16[256,1024]{1,0:T(8,128)(2,1)S(1)}, bf16[256,1024]{1,0:T(8,128)(2,1)}, u32[]{:S(2)}) copy-start(bf16[256,1024]{1,0:T(8,128)(2,1)} %param.28) | copy-start | bytes 1572868
  526.1 23.6 %copy-start.15 = (s32[2048]{0:T(1024)S(1)}, s32[2048]{0:T(1024)}, u32[]{:S(2)}) copy-start(s32[2048]{0:T(1024)} %copy-done.14) | copy-start | bytes 24580
  551.3 4.4 copy-start.16
  584.9 7.1 copy-start.2
  631.4 7.1 copy-start.2
  678.6 7.1 copy-start.2
  725.9 7.1 copy-start.2
  737.8 10.7 copy-start.25
  737.9 10.7 copy-start.35
  748.5 8.5 copy-start.11
  748.5 8.5 copy-start.41
  759.1 12.0 %copy-start.9 = (bf16[4,512,4,64]{1,3,2,0:T(8,128)(2,1)S(1)}, bf16[4,512,4,64]{1,3,2,0:T(8,128)(2,1)}, u32[]{:S(2)}) copy-start(bf16[4,512,4,64]{1,3,2,0:T(8,128)(2,1)} %get-tuple-element.119) | copy-start | bytes 3145732
  759.2 12.4 %copy-start.40 = (bf16[1024]{0:T(1024)(128)(2,1)S(1)}, bf16[1024]{0:T(1024)(128)(2,1)}, u32[]{:S(2)}) copy-start(bf16[1024]{0:T(1024)(128)(2,1)} %get-tuple-element.255) | copy-start | bytes 6148
  759.2 261.1 %reduce-scatter.8.cloned.1.call-start = ((), (), s32[]{:S(2)}) async-start(), calls=%async_computation.9 | async-start | bytes 5242880 | tf_op jit(solution)/shard_map/reduce_scatter | solution.py:210
  974.3 10.9 %copy-start.13 = (bf16[1024,1024]{1,0:T(8,128)(2,1)S(1)}, bf16[1024,1024]{1,0:T(8,128)(2,1)}, u32[]{:S(2)}) copy-start(bf16[1024,1024]{1,0:T(8,128)(2,1)} %get-tuple-element.254) | copy-start | bytes 6291460
  980.0 42.9 %copy-start.29 = (f32[1024]{0:T(1024)S(1)}, f32[1024]{0:T(1024)}, u32[]{:S(2)}) copy-start(f32[1024]{0:T(1024)} %get-tuple-element.260) | copy-start | bytes 12292
  980.0 42.9 %copy-start.30 = (f32[1024]{0:T(1024)S(1)}, f32[1024]{0:T(1024)}, u32[]{:S(2)}) copy-start(f32[1024]{0:T(1024)} %get-tuple-element.191) | copy-start | bytes 12292
  980.0 42.9 %copy-start.31 = (f32[1024]{0:T(1024)S(1)}, f32[1024]{0:T(1024)}, u32[]{:S(2)}) copy-start(f32[1024]{0:T(1024)} %get-tuple-element.199) | copy-start | bytes 12292
  980.0 42.9 %copy-start.32 = (f32[1024]{0:T(1024)S(1)}, f32[1024]{0:T(1024)}, u32[]{:S(2)}) copy-start(f32[1024]{0:T(1024)} %get-tuple-element.277) | copy-start | bytes 12292
  985.2 84.0 %copy-start.1 = (bf16[1024,1024]{1,0:T(8,128)(2,1)S(1)}, bf16[1024,1024]{1,0:T(8,128)(2,1)}, u32[]{:S(2)}) copy-start(bf16[1024,1024]{1,0:T(8,128)(2,1)} %param.34) | copy-start | bytes 6291460
  (17 other events, 58.8 us)
Sparse Core Ops, SparseCore 0:
  9.6 37.1 all-gather.3
  236.7 85.4 all-reduce.5
  324.4 34.6 all-gather.5
  409.1 44.6 reduce-scatter.5
  456.7 44.5 reduce-scatter.3
  507.4 34.4 all-gather.7
  759.3 214.9 all-reduce.7
  976.8 43.4 reduce-scatter.7
where the time goes:
time: 1080 us
  waiting for transfers between devices  413 us (38%)
  matrix products  274 us (25%)
  other arithmetic  272 us (25%)
  blocking collectives  62.7 us (6%)
  local copies, waits for them, and re-layouts  38.1 us (4%)
  between operations  15.6 us (1%)
    psum x1, waiting for transfers between devices, per_device(): lax.psum(grad_qkv.astype(jnp.bfloat16), 'dp').astype(jnp.float32)  179 us
    psum x1, waiting for transfers between devices, per_device(): lax.psum(attn_part.astype(jnp.bfloat16), 'mp').astype(jnp.float32)  81.7 us
    reduce_sum x2, other arithmetic, normalize(): centred = stream - jnp.mean(stream, axis=1, keepdims=True)  70.7 us
    reduce_scatter x2, waiting for transfers between devices, own_rows(): lax.psum_scatter(partial_sum.astype(jnp.bfloat16), 'mp', scatter_dimensio...  57.7 us
    dot_general x4, matrix products, block_step(): jnp.einsum('qhd,khd->hqk', grad_part, value_rows, preferred_element_type=...  45.8 us
    reduce_scatter x1, waiting for transfers between devices, per_device(): lax.psum_scatter(mlp_part.astype(jnp.bfloat16), 'mp', scatter_dimension=0...  44.3 us
    convert_element_type x4, other arithmetic, block_step(): grad_scores = (probs * (grad_probs - centre)).astype(jnp.bfloat16)  44.1 us
    psum x1, blocking collectives, per_device(): lax.psum((square_sums, grad_ln1_gain, grad_ln1_bias, grad_out_bias, grad_...  40.1 us
  transfers between devices with their start and end apart: 8, of which 7 were waited for; matrix products, arithmetic and copies ran while one was open for 11% of the time, Pallas kernels for 0%

commit v1 on v0

v1 whole, which is shorter than its diff:
```python
import functools
import math

import jax
import jax.numpy as jnp
from jax import lax
from jax.experimental import pallas as pl
from jax.experimental.pallas import tpu as pltpu
from jax.sharding import PartitionSpec as P

HD = 64
EPS = 1e-06
MASKED = -1e30
F32 = jnp.float32
BF16 = jnp.bfloat16
NT = (((1,), (1,)), ((), ()))
TN = (((0,), (0,)), ((), ()))
NN = (((1,), (0,)), ((), ()))
VMEM_LIMIT = 56 * 1024 * 1024


def mxu(left, right, dims):
    return lax.dot_general(left, right, dims, preferred_element_type=F32)


def whole(shape):
    return pl.BlockSpec(shape, lambda *_: (0,) * len(shape))


def scalars():
    return pl.BlockSpec(memory_space=pltpu.SMEM)


def call(body, grid, in_specs, out_specs, out_shape, flops, moved, scratch=(), transcendentals=0):
    return pl.pallas_call(
        body,
        grid=grid,
        in_specs=in_specs,
        out_specs=out_specs,
        out_shape=out_shape,
        scratch_shapes=list(scratch),
        compiler_params=pltpu.CompilerParams(
            dimension_semantics=("arbitrary",) * len(grid), vmem_limit_bytes=VMEM_LIMIT
        ),
        cost_estimate=pl.CostEstimate(
            flops=int(flops), bytes_accessed=int(moved), transcendentals=int(transcendentals)
        ),
    )


def like(shape, dtype):
    return jax.ShapeDtypeStruct(shape, dtype)


def item_ends(lengths_ref, item_count):
    ends, total = [], 0
    for item in range(item_count):
        total = total + lengths_ref[item]
        ends.append(total)
    return ends


def segment_of(rows, ends):
    segment = jnp.zeros(rows.shape, jnp.int32)
    for end in ends:
        segment = segment + jnp.where(rows >= end, 1, 0)
    return segment


def scalar_segment(row, ends):
    segment = jnp.int32(0)
    for end in ends:
        segment = segment + jnp.where(row >= end, 1, 0)
    return segment


def valid_column(lengths_ref, item_count, first_row, row_count):
    rows = first_row + lax.broadcasted_iota(jnp.int32, (row_count, 1), 0)
    return jnp.where(rows < item_ends(lengths_ref, item_count)[-1], 1.0, 0.0).astype(F32)


def normalize(stream):
    centred = stream - jnp.mean(stream, axis=1, keepdims=True)
    rstd = lax.rsqrt(jnp.mean(centred * centred, axis=1, keepdims=True) + EPS)
    return centred * rstd, rstd


def norm_back(gradient, scaled, gain, rstd):
    spread = gradient * gain
    first = jnp.mean(spread, axis=1, keepdims=True)
    second = jnp.mean(spread * scaled, axis=1, keepdims=True)
    return rstd * (spread - first - scaled * second)


def column_sum(array):
    return jnp.sum(array, axis=0, keepdims=True)


def sin_cos(angle):
    turns = jnp.floor(angle * (2.0 / math.pi) + 0.5)
    rest = angle - turns * 1.5703125
    rest = rest - turns * 4.837512969970703125e-4
    rest = rest - turns * 7.54978995489188216e-8
    square = rest * rest
    sine = rest + rest * square * (
        -1.6666654611e-1 + square * (8.3321608736e-3 + square * -1.9515295891e-4)
    )
    cosine = (
        1.0
        - 0.5 * square
        + square
        * square
        * (
            4.166664568298827e-2
            + square * (-1.388731625493765e-3 + square * 2.443315711809948e-5)
        )
    )
    quarter = turns.astype(jnp.int32)
    odd = (quarter & 1) == 1
    sine_flip = (quarter & 2) != 0
    cosine_flip = ((quarter + 1) & 2) != 0
    first = jnp.where(odd, cosine, sine)
    second = jnp.where(odd, sine, cosine)
    return jnp.where(sine_flip, -first, first), jnp.where(cosine_flip, -second, second)


def encode_body(item_count, lengths, ratios, place, tokens, freq, gain, bias, stream_out, normed_out):
    rows_here, width = tokens.shape
    row = (
        place[0] * (rows_here * pl.num_programs(0))
        + pl.program_id(0) * rows_here
        + lax.broadcasted_iota(jnp.int32, (rows_here, 1), 0)
    )
    position = jnp.zeros((rows_here, 1), jnp.int32)
    ratio = jnp.zeros((rows_here, 1), F32)
    start = 0
    for item in range(item_count):
        end = start + lengths[item]
        inside = (row >= start) & (row < end)
        position = jnp.where(inside, row - start, position)
        ratio = jnp.where(inside, ratios[item], ratio)
        start = end
    angle = (position.astype(F32) * ratio) * freq[...]
    sine, cosine = sin_cos(angle)
    stream = tokens[...].astype(F32) + jnp.concatenate([sine, cosine], axis=1)
    stream_out[...] = stream
    scaled, _ = normalize(stream)
    normed_out[...] = (scaled * gain[...] + bias[...]).astype(BF16)


def encode(lengths, ratios, place, tokens, gain, bias):
    rows, width = tokens.shape
    half = width // 2
    tile = min(128, rows)
    freq = jnp.exp(jnp.arange(half, dtype=jnp.int32).astype(F32) * (-math.log(10000.0) / half))[None]
    body = functools.partial(encode_body, lengths.shape[0])
    block = pl.BlockSpec((tile, width), lambda i: (i, 0))
    return call(
        body,
        (rows // tile,),
        [scalars(), scalars(), scalars(), block, whole((1, half)), whole((1, width)), whole((1, width))],
        [block, block],
        [like((rows, width), F32), like((rows, width), BF16)],
        60 * rows * width,
        8 * rows * width,
    )(lengths, ratios, place, tokens, freq, gain, bias)


def tile_range(tile, tile_rows, own_rows, place, ends):
    span = max(tile_rows, own_rows)
    group = tile * tile_rows // span
    within = tile * tile_rows - group * span
    piece = group * (span // own_rows)
    first = ((piece ^ place) * own_rows) // span * span + within
    return scalar_segment(first, ends), scalar_segment(first + tile_rows - 1, ends)


def share_item(range_a, range_b, item_count):
    low = jnp.maximum(range_a[0], range_b[0])
    high = jnp.minimum(range_a[1], range_b[1])
    return (low <= high) & (low < item_count)


def marks(tile, tile_rows, own_rows, place, ends):
    rows = tile * tile_rows + lax.broadcasted_iota(jnp.int32, (tile_rows, HD), 0)
    lane = lax.broadcasted_iota(jnp.int32, (tile_rows, HD), 1)
    segment = segment_of(rows ^ (place * own_rows), ends)
    same = segment == lane
    query_marks = jnp.where(same, 1.0, 0.0).astype(BF16)
    key_marks = jnp.where(same | (lane > len(ends)), 0.0, MASKED).astype(BF16)
    return query_marks, key_marks


def attend_body(
    item_count, heads, tile, piece_count, lengths, place_ref, *refs
):
    pieces = refs[:piece_count]
    out, lse_out = refs[piece_count : piece_count + 2]
    qa, ka, vt, acc, top = refs[piece_count + 2 :]
    own_rows = pieces[0].shape[0]
    rows = own_rows * piece_count
    tiles = rows // tile
    width = heads * HD
    place = place_ref[0]
    ends = item_ends(lengths, item_count)
    part = min(tile, own_rows)
    for t in range(tiles):
        query_marks, key_marks = marks(t, tile, own_rows, place, ends)
        for h in range(heads):
            for s in range(tile // part):
                row = t * tile + s * part
                ref = pieces[row // own_rows]
                here = pl.ds(row % own_rows, part)
                there = slice(s * part, (s + 1) * part)
                query = ref[here, h * HD : (h + 1) * HD] * jnp.asarray(HD**-0.5, BF16)
                key = ref[here, width + h * HD : width + (h + 1) * HD]
                value = ref[here, 2 * width + h * HD : 2 * width + (h + 1) * HD]
                qa[h, t, there, :] = jnp.concatenate([query, query_marks[there]], axis=1)
                ka[h, t, there, :] = jnp.concatenate([key, key_marks[there]], axis=1)
                ones = jnp.ones((part, HD), BF16)
                vt[h, t, :, there] = jnp.concatenate([value, ones], axis=1).T

    def query_tile(i, carry):
        range_i = tile_range(i, tile, own_rows, place, ends)

        acc[...] = jnp.zeros(acc.shape, F32)
        top[...] = jnp.full(top.shape, -3e38, F32)

        def key_tile(j, inner):
            @pl.when(share_item(range_i, tile_range(j, tile, own_rows, place, ends), item_count))
            def _():
                scores = [mxu(ka[h, j], qa[h, i], NT) for h in range(heads)]
                for h in range(heads):
                    old = top[h]
                    new = jnp.maximum(old, jnp.max(scores[h], axis=0, keepdims=True))
                    probs = jnp.exp(scores[h] - new).astype(BF16)
                    top[h] = new
                    acc[h] = acc[h] * jnp.exp(old - new) + mxu(vt[h, j], probs, NN)

            return inner

        lax.fori_loop(0, tiles, key_tile, 0)
        for h in range(heads):
            total = jnp.maximum(acc[h, HD : HD + 1, :], 1e-30)
            lse_out[h, i] = top[h] + jnp.log(total)
        mixed = [acc[h, :HD, :] / jnp.maximum(acc[h, HD : HD + 1, :], 1e-30) for h in range(heads)]
        here = pl.ds(pl.multiple_of(i * tile, tile), tile)
        for h in range(0, heads, 2):
            group = mixed[h : h + 2]
            both = jnp.concatenate(group, axis=0) if len(group) > 1 else group[0]
            out[here, h * HD : (h + len(group)) * HD] = both.T.astype(BF16)
        return carry

    lax.fori_loop(0, tiles, query_tile, 0)


def attend(lengths, place, pieces):
    own_rows, width3 = pieces[0].shape
    width = width3 // 3
    heads = width // HD
    rows = own_rows * len(pieces)
    tile = min(256, rows)
    tiles = rows // tile
    body = functools.partial(attend_body, lengths.shape[0], heads, tile, len(pieces))
    return call(
        body,
        (1,),
        [scalars(), scalars()] + [whole((own_rows, width3))] * len(pieces),
        [whole((rows, width)), whole((heads, tiles, 1, tile))],
        [like((rows, width), BF16), like((heads, tiles, 1, tile), F32)],
        rows * rows * width * 2,
        10 * rows * width,
        [
            pltpu.VMEM((heads, tiles, tile, 2 * HD), BF16),
            pltpu.VMEM((heads, tiles, tile, 2 * HD), BF16),
            pltpu.VMEM((heads, tiles, 2 * HD, tile), BF16),
            pltpu.VMEM((heads, 2 * HD, tile), F32),
            pltpu.VMEM((heads, 1, tile), F32),
        ],
    )(lengths, place, *pieces)


def attend_back_body(item_count, heads, tile, piece_count, lengths, place_ref, *refs):
    pieces = refs[:piece_count]
    grads = refs[piece_count : 2 * piece_count]
    mixed, lse, out = refs[2 * piece_count : 2 * piece_count + 3]
    qa, ka, kt, vals, dos, delta, dk, dv, dqt = refs[2 * piece_count + 3 :]
    own_rows = pieces[0].shape[0]
    rows = own_rows * piece_count
    tiles = rows // tile
    width = heads * HD
    place = place_ref[0]
    ends = item_ends(lengths, item_count)
    part = min(tile, own_rows)
    scale = HD**-0.5
    for t in range(tiles):
        query_marks, key_marks = marks(t, tile, own_rows, place, ends)
        for s in range(tile // part):
            row = t * tile + s * part
            ref = pieces[row // own_rows]
            grad_ref = grads[row // own_rows]
            here = pl.ds(row % own_rows, part)
            there = slice(s * part, (s + 1) * part)
            for h in range(heads):
                query = ref[here, h * HD : (h + 1) * HD] * jnp.asarray(scale, BF16)
                key = ref[here, width + h * HD : width + (h + 1) * HD]
                qa[h, t, there, :] = jnp.concatenate([query, query_marks[there]], axis=1)
                ka[h, t, there, :] = jnp.concatenate([key, key_marks[there]], axis=1)
                vals[h, t, there, :] = ref[here, 2 * width + h * HD : 2 * width + (h + 1) * HD]
                dos[h, t, there, :] = grad_ref[here, h * HD : (h + 1) * HD]
            for h in range(0, heads, 2):
                count = min(2, heads - h)
                columns = slice(h * HD, (h + count) * HD)
                keys = ref[here, width + h * HD : width + (h + count) * HD].T
                weighed = (
                    grad_ref[here, columns].astype(F32)
                    * mixed[pl.ds(row, part), columns].astype(F32)
                ).T
                for k in range(count):
                    kt[h + k, t, :, there] = keys[k * HD : (k + 1) * HD]
                    delta[h + k, t, :, there] = column_sum(weighed[k * HD : (k + 1) * HD])
    dqt[...] = jnp.zeros(dqt.shape, F32)

    def key_tile(j, carry):
        range_j = tile_range(j, tile, own_rows, place, ends)
        dk[...] = jnp.zeros(dk.shape, F32)
        dv[...] = jnp.zeros(dv.shape, F32)

        def query_tile(i, inner):
            @pl.when(share_item(range_j, tile_range(i, tile, own_rows, place, ends), item_count))
            def _():
                for h in range(heads):
                    scores = mxu(ka[h, j], qa[h, i], NT)
                    grad_probs = mxu(vals[h, j], dos[h, i], NT)
                    probs = jnp.exp(scores - lse[h, i])
                    grad_scores = (probs * (grad_probs - delta[h, i])).astype(BF16)
                    dv[h] += mxu(probs.astype(BF16), dos[h, i], NN)
                    dk[h] += mxu(grad_scores, qa[h, i], NN)
                    dqt[h, i] += mxu(kt[h, j], grad_scores, NN)

            return inner

        lax.fori_loop(0, tiles, query_tile, 0)
        here = pl.ds(pl.multiple_of(j * tile, tile), tile)
        for h in range(0, heads, 2):
            count = min(2, heads - h)
            keys = [dk[h + k][:, :HD] for k in range(count)]
            values = [dv[h + k] for k in range(count)]
            if count > 1:
                keys, values = [jnp.concatenate(keys, axis=1)], [jnp.concatenate(values, axis=1)]
            out[here, width + h * HD : width + (h + count) * HD] = keys[0].astype(BF16)
            out[here, 2 * width + h * HD : 2 * width + (h + count) * HD] = values[0].astype(BF16)
        return carry

    lax.fori_loop(0, tiles, key_tile, 0)
    for t in range(tiles):
        for h in range(0, heads, 2):
            count = min(2, heads - h)
            both = [dqt[h + k, t] for k in range(count)]
            both = jnp.concatenate(both, axis=0) if count > 1 else both[0]
            out[t * tile : (t + 1) * tile, h * HD : (h + count) * HD] = (both.T * scale).astype(BF16)


def attend_back(lengths, place, pieces, grads, mixed, lse):
    own_rows, width3 = pieces[0].shape
    width = width3 // 3
    heads = width // HD
    rows = own_rows * len(pieces)
    tile = min(256, rows)
    tiles = rows // tile
    body = functools.partial(attend_back_body, lengths.shape[0], heads, tile, len(pieces))
    return call(
        body,
        (1,),
        [scalars(), scalars()]
        + [whole((own_rows, width3))] * len(pieces)
        + [whole((own_rows, width))] * len(pieces)
        + [whole((rows, width)), whole((heads, tiles, 1, tile))],
        whole((rows, width3)),
        like((rows, width3), BF16),
        rows * rows * width * 5,
        16 * rows * width,
        [
            pltpu.VMEM((heads, tiles, tile, 2 * HD), BF16),
            pltpu.VMEM((heads, tiles, tile, 2 * HD), BF16),
            pltpu.VMEM((heads, tiles, HD, tile), BF16),
            pltpu.VMEM((heads, tiles, tile, HD), BF16),
            pltpu.VMEM((heads, tiles, tile, HD), BF16),
            pltpu.VMEM((heads, tiles, 1, tile), F32),
            pltpu.VMEM((heads, tile, 2 * HD), F32),
            pltpu.VMEM((heads, tile, HD), F32),
            pltpu.VMEM((heads, tiles, HD, tile), F32),
        ],
    )(lengths, place, *pieces, *grads, mixed, lse)


def branch_body(item_count, piece_count, lengths, place, *refs):
    mixed = refs[:piece_count]
    weights = refs[piece_count : 2 * piece_count]
    stream0, shift, gain, bias, stream1, normed, squares = refs[2 * piece_count :]
    tile = stream0.shape[0]
    attn = shift[...]
    for left, right in zip(mixed, weights):
        attn = attn + mxu(left[...], right[...], NN)
    first = place[0] * (tile * pl.num_programs(0)) + pl.program_id(0) * tile
    valid = valid_column(lengths, item_count, first, tile)
    stream = stream0[...] + attn
    stream1[...] = stream
    scaled, _ = normalize(stream)
    normed[...] = (scaled * gain[...] + bias[...]).astype(BF16)

    @pl.when(pl.program_id(0) == 0)
    def _():
        squares[...] = jnp.zeros(squares.shape, F32)

    squares[...] += column_sum(valid * attn * attn)


def branch(lengths, place, mixed, weights, stream0, shift, gain, bias):
    rows, width = stream0.shape
    tile = min(256, rows)
    count = len(mixed)
    block = pl.BlockSpec((tile, width), lambda i: (i, 0))
    narrow = pl.BlockSpec((tile, mixed[0].shape[1]), lambda i: (i, 0))
    line = whole((1, width))
    return call(
        functools.partial(branch_body, lengths.shape[0], count),
        (rows // tile,),
        [scalars(), scalars()]
        + [narrow] * count
        + [whole(weights[0].shape)] * count
        + [block, line, line, line],
        [block, block, line],
        [like((rows, width), F32), like((rows, width), BF16), like((1, width), F32)],
        2 * rows * width * width,
        rows * width * 12 + 2 * width * width,
    )(lengths, place, *mixed, *weights, stream0, shift, gain, bias)


def feed_body(normed, grad_mlp, w_up, up_bias, w_down, act_out, upin_out, mlp_out, norm_out, bias_out):
    hidden = w_up.shape[1]
    chunk = min(256, hidden)
    left, grad = normed[...], grad_mlp[...]
    mlp = norm = None

    @pl.when(pl.program_id(0) == 0)
    def _():
        bias_out[...] = jnp.zeros(bias_out.shape, F32)

    for c in range(0, hidden, chunk):
        here = slice(c, c + chunk)
        up = mxu(left, w_up[:, here], NN) + up_bias[:, here]
        grad_act = mxu(grad, w_down[here, :], NT)
        size = jnp.abs(up)
        decay = jnp.exp(-0.5 * up * up)
        t = 1.0 / (1.0 + (0.3275911 * 0.7071067811865476) * size)
        series = t * (
            0.254829592
            + t * (-0.284496736 + t * (1.421413741 + t * (-1.453152027 + t * 1.061405429)))
        )
        tail = 0.5 * series * decay
        share = jnp.where(up >= 0.0, 1.0 - tail, tail)
        act = (up * share).astype(BF16)
        upin = ((share + up * decay * 0.3989422804014327) * grad_act).astype(BF16)
        act_out[:, here] = act
        upin_out[:, here] = upin
        bias_out[:, here] += column_sum(upin.astype(F32))
        mlp_part = mxu(act, w_down[here, :], NN)
        norm_part = mxu(upin, w_up[:, here], NT)
        mlp = mlp_part if mlp is None else mlp + mlp_part
        norm = norm_part if norm is None else norm + norm_part
    mlp_out[...] = mlp.astype(BF16)
    norm_out[...] = norm.astype(BF16)


def feed(normed, grad_mlp, w_up, up_bias, w_down):
    rows, width = normed.shape
    hidden = w_up.shape[1]
    tile = min(256, rows)
    block = pl.BlockSpec((tile, width), lambda i: (i, 0))
    wide = pl.BlockSpec((tile, hidden), lambda i: (i, 0))
    return call(
        feed_body,
        (rows // tile,),
        [block, block, whole(w_up.shape), whole((1, hidden)), whole(w_down.shape)],
        [wide, wide, block, block, whole((1, hidden))],
        [
            like((rows, hidden), BF16),
            like((rows, hidden), BF16),
            like((rows, width), BF16),
            like((rows, width), BF16),
            like((1, hidden), F32),
        ],
        8 * rows * width * hidden,
        12 * rows * width + 4 * width * hidden,
        transcendentals=rows * hidden,
    )(normed, grad_mlp, w_up, up_bias, w_down)


def outer_body(piece_count, *refs):
    left, right, out = refs[:piece_count], refs[piece_count : 2 * piece_count], refs[-1]
    total = None
    for a, b in zip(left, right):
        term = mxu(a[...], b[...], TN)
        total = term if total is None else total + term
    out[...] = total.astype(out.dtype)


def outer(left, right):
    rows, depth = left[0].shape
    width = right[0].shape[1]
    tile = min(256, depth)
    count = len(left)
    return call(
        functools.partial(outer_body, count),
        (depth // tile,),
        [pl.BlockSpec((rows, tile), lambda i: (0, i))] * count + [whole((rows, width))] * count,
        pl.BlockSpec((tile, width), lambda i: (i, 0)),
        like((depth, width), BF16),
        2 * count * rows * depth * width,
        2 * count * rows * (depth + width) + 2 * depth * width,
    )(*left, *right)


def second_back_body(item_count, piece_count, lengths, place, half_a, half_b, stream1, cotangent, gain, *refs):
    weights = refs[:piece_count]
    grad_out, attn_out = refs[piece_count : piece_count + 2]
    mixed_out = refs[piece_count + 2 : 2 * piece_count + 2]
    sums = refs[-1]
    tile = stream1.shape[0]
    first = place[0] * (tile * pl.num_programs(0)) + pl.program_id(0) * tile
    valid = valid_column(lengths, item_count, first, tile)
    grad_norm = half_a[...].astype(F32) + half_b[...].astype(F32)
    scaled, rstd = normalize(stream1[...])
    grad = valid * cotangent[...].astype(F32) + norm_back(grad_norm, scaled, gain[...], rstd)
    grad_out[...] = grad
    rounded = grad.astype(BF16)
    attn_out[...] = rounded

    @pl.when(pl.program_id(0) == 0)
    def _():
        sums[...] = jnp.zeros(sums.shape, F32)

    sums[0:1] += column_sum(grad_norm * scaled)
    sums[1:2] += column_sum(grad_norm)
    sums[2:3] += column_sum(rounded.astype(F32))
    for weight, mixed in zip(weights, mixed_out):
        mixed[...] = mxu(rounded, weight[...], NT).astype(BF16)


def second_back(lengths, place, half_a, half_b, stream1, cotangent, gain, weights):
    rows, width = stream1.shape
    tile = min(256, rows)
    count = len(weights)
    depth = weights[0].shape[0]
    block = pl.BlockSpec((tile, width), lambda i: (i, 0))
    narrow = pl.BlockSpec((tile, depth), lambda i: (i, 0))
    results = call(
        functools.partial(second_back_body, lengths.shape[0], count),
        (rows // tile,),
        [scalars(), scalars(), block, block, block, block, whole((1, width))]
        + [whole(weights[0].shape)] * count,
        [block, block] + [narrow] * count + [whole((8, width))],
        [like((rows, width), F32), like((rows, width), BF16)]
        + [like((rows, depth), BF16)] * count
        + [like((8, width), F32)],
        2 * rows * width * width,
        rows * width * 20 + 2 * width * width,
    )(lengths, place, half_a, half_b, stream1, cotangent, gain, *weights)
    return results[0], results[1], results[2:-1], results[-1][:3]


def output_body(item_count, lengths, place, half_a, half_b, shift, stream1, cotangent, out, sums):
    tile = stream1.shape[0]
    first = place[0] * (tile * pl.num_programs(0)) + pl.program_id(0) * tile
    valid = valid_column(lengths, item_count, first, tile)
    mlp = half_a[...].astype(F32) + half_b[...].astype(F32) + shift[...]
    stream2 = stream1[...] + mlp
    out[...] = (valid * stream2).astype(BF16)

    @pl.when(pl.program_id(0) == 0)
    def _():
        sums[...] = jnp.zeros(sums.shape, F32)

    sums[0:1] += column_sum(valid * stream2 * stream2)
    sums[1:2] += column_sum(valid * mlp * mlp)
    sums[2:3] += column_sum((valid * cotangent[...].astype(F32)).astype(BF16).astype(F32))
    sums[3:4] += jnp.broadcast_to(column_sum(valid), (1, stream1.shape[1]))


def output_end(lengths, place, half_a, half_b, shift, stream1, cotangent):
    rows, width = stream1.shape
    tile = min(256, rows)
    block = pl.BlockSpec((tile, width), lambda i: (i, 0))
    out, sums = call(
        functools.partial(output_body, lengths.shape[0]),
        (rows // tile,),
        [scalars(), scalars(), block, block, whole((1, width)), block, block],
        [block, whole((8, width))],
        [like((rows, width), BF16), like((8, width), F32)],
        12 * rows * width,
        rows * width * 12,
    )(lengths, place, half_a, half_b, shift, stream1, cotangent)
    return out, sums[:4]


def input_body(half_a, half_b, stream0, grad_stream1, gain, out, sums):
    grad_norm = half_a[...].astype(F32) + half_b[...].astype(F32)
    scaled, rstd = normalize(stream0[...])
    out[...] = grad_stream1[...] + norm_back(grad_norm, scaled, gain[...], rstd)

    @pl.when(pl.program_id(0) == 0)
    def _():
        sums[...] = jnp.zeros(sums.shape, F32)

    sums[0:1] += column_sum(grad_norm * scaled)
    sums[1:2] += column_sum(grad_norm)


def input_end(half_a, half_b, stream0, grad_stream1, gain):
    rows, width = stream0.shape
    tile = min(256, rows)
    block = pl.BlockSpec((tile, width), lambda i: (i, 0))
    out, sums = call(
        input_body,
        (rows // tile,),
        [block, block, block, block, whole((1, width))],
        [block, whole((8, width))],
        [like((rows, width), F32), like((8, width), F32)],
        12 * rows * width,
        rows * width * 16,
    )(half_a, half_b, stream0, grad_stream1, gain)
    return out, sums[:2]


def swap(array, axis, bit):
    return lax.ppermute(array, axis, [(i, i ^ bit) for i in range(lax.axis_size(axis))])


def gather(own, axis="mp"):
    pieces = {0: own}
    bit = lax.axis_size(axis) // 2
    while bit:
        for p in sorted(pieces):
            pieces[p | bit] = swap(pieces[p], axis, bit)
        bit //= 2
    return [pieces[p] for p in range(len(pieces))]


def exchange(parts, axis="mp"):
    return [parts[0]] + [swap(parts[p], axis, p) for p in range(1, len(parts))]


def add(left, right):
    return (left.astype(F32) + right.astype(F32)).astype(left.dtype)


def scatter_sum(parts, axis="mp"):
    count, bit = len(parts), 1
    kept = dict(enumerate(parts))
    while bit < count:
        arrived = {p: swap(kept[p | bit], axis, bit) for p in kept if not p & bit}
        if 2 * bit == count:
            return kept[0], arrived[0]
        kept = {p: add(kept[p], arrived[p]) for p in arrived}
        bit *= 2
    return kept[0], jnp.zeros_like(kept[0])


def total(array, axis):
    bit = 1
    while bit < lax.axis_size(axis):
        array = array + swap(array, axis, bit)
        bit *= 2
    return array


def per_device(
    tokens, cotangent, item_lengths, gsd_ratio, ln1_gain, ln1_bias, w_qkv, qv_bias, w_out, out_bias,
    ln2_gain, ln2_bias, w_up, up_bias, w_down, down_bias,
):
    own_rows, width = tokens.shape
    mp_count = lax.axis_size("mp")
    mine = lax.axis_index("mp")
    place = mine.astype(jnp.int32)[None]
    depth = w_qkv.shape[1]
    item_count = item_lengths.shape[0]
    gain1, bias1 = ln1_gain.astype(F32)[None], ln1_bias.astype(F32)[None]
    gain2, bias2 = ln2_gain[None], ln2_bias[None]

    stream0, normed1_own = encode(item_lengths, gsd_ratio, place, tokens, gain1, bias1)
    normed1 = gather(normed1_own)
    w_flat = w_qkv.reshape(3 * depth, width)
    shift = jnp.concatenate([qv_bias[0], jnp.zeros((depth,), F32), qv_bias[1]])[None]
    qkv = [(mxu(piece, w_flat, NT) + shift).astype(BF16) for piece in normed1]

    rows_here = mine * own_rows + jnp.arange(own_rows, dtype=jnp.int32)
    valid = (rows_here < jnp.sum(item_lengths)).astype(F32)[:, None]
    grad_mlp_own = (valid * cotangent.astype(F32)).astype(BF16)
    w_out_all = gather(w_out)
    grad_mlp = gather(grad_mlp_own)

    attended, logsum = attend(item_lengths, place, qkv)
    mixed = exchange([attended[p * own_rows : (p + 1) * own_rows] for p in range(mp_count)])
    stream1, normed2_own, attn_squares = branch(
        item_lengths, place, mixed, w_out_all, stream0, out_bias[None], gain2, bias2
    )
    normed2 = gather(normed2_own)

    fed = [feed(normed2[p], grad_mlp[p], w_up, up_bias[None], w_down) for p in range(mp_count)]
    norm2_a, norm2_b = scatter_sum([f[3] for f in fed])
    mlp_a, mlp_b = scatter_sum([f[2] for f in fed])
    grad_down = outer([f[0] for f in fed], grad_mlp)
    grad_up = outer(normed2, [f[1] for f in fed])
    grad_up_bias = functools.reduce(jnp.add, [f[4] for f in fed])

    grad_stream1, grad_attn, grad_mixed, second_sums = second_back(
        item_lengths, place, norm2_a, norm2_b, stream1, cotangent, gain2, w_out_all
    )
    output, output_sums = output_end(
        item_lengths, place, mlp_a, mlp_b, down_bias[None], stream1, cotangent
    )

    grads = exchange(list(grad_mixed))
    out_a, out_b = scatter_sum([outer([m], [grad_attn]) for m in mixed])
    grad_out_weight = add(out_a, out_b)
    grad_proj = attend_back(item_lengths, place, qkv, grads, attended, logsum)
    proj_parts = [grad_proj[p * own_rows : (p + 1) * own_rows] for p in range(mp_count)]
    norm1_a, norm1_b = scatter_sum([mxu(part, w_flat, NN).astype(BF16) for part in proj_parts])
    grad_qkv = outer(proj_parts, normed1)
    proj_sums = jnp.sum(grad_proj.astype(F32), axis=0)
    input_grad, first_sums = input_end(norm1_a, norm1_b, stream0, grad_stream1, gain1)

    grad_down, grad_up = lax.psum((grad_down, grad_up), "dp")
    grad_qkv, grad_out_weight = lax.psum((grad_qkv, grad_out_weight), "dp")
    rows = jnp.concatenate([first_sums, second_sums, output_sums, attn_squares], axis=0)
    rows = total(rows, "mp")
    flat = jnp.concatenate([rows.reshape(-1), grad_up_bias[0], proj_sums])
    flat = jnp.pad(flat, (0, -flat.size % 1024))
    flat = total(flat.reshape(-1, 128), "dp").reshape(-1)
    rows = flat[: rows.size].reshape(rows.shape)
    up_sums = flat[rows.size : rows.size + up_bias.shape[0]]
    proj_sums = flat[rows.size + up_bias.shape[0] :][: 3 * depth]
    squares = jnp.stack([jnp.sum(rows[5]), jnp.sum(rows[9]), jnp.sum(rows[6])])
    stats = jnp.sqrt(squares / (rows[8, 0] * width))
    return (
        output,
        input_grad,
        rows[0],
        rows[1],
        grad_qkv.astype(F32).reshape(3, depth, width),
        jnp.stack([proj_sums[:depth], proj_sums[2 * depth :]]),
        grad_out_weight.astype(F32),
        rows[4],
        rows[2],
        rows[3],
        grad_up.astype(F32),
        up_sums,
        grad_down.astype(F32),
        rows[7],
        stats,
    )


def solution(mesh):
    rows, one = P(("dp", "mp"), None), P()
    placed = (
        rows, rows, P("dp"), P("dp"), one, one, P(None, "mp", None), P(None, "mp"), P("mp", None), one,
        one, one, P(None, "mp"), P("mp"), P("mp", None), one,
    )
    results = (
        rows, rows, one, one, P(None, "mp", None), P(None, "mp"), P("mp", None), one,
        one, one, P(None, "mp"), P("mp"), P("mp", None), one, one,
    )
    return jax.shard_map(per_device, mesh=mesh, in_specs=placed, out_specs=results, check_vma=False)
```

time: 1080 us -> 538 us (0.50)
  matrix products: 274 us -> 16.4 us
  other arithmetic: 272 us -> 28.6 us
  Pallas kernels: 0 us -> 151 us
  waiting for transfers between devices: 413 us -> 262 us
  blocking collectives: 62.7 us -> 0 us
  starting transfers between devices: 0.79 us -> 41.2 us
  local copies, waits for them, and re-layouts: 38.1 us -> 15.4 us
    dot_general x40 -> x8, matrix products: 274 us -> 16.4 us  [mxu(): return lax.dot_general(left, right, dims, preferred_element_type=F32)]
    pallas_call x0 -> x18, Pallas kernels: none -> 151 us  [the longest x4 41.7 us: feed(): call(feed_body, (rows // tile,), [block, block, whole(w_up.shape), whole(...]
    reduce_sum x18 -> x3, other arithmetic: 143 us -> 3.03 us  [the longest x1 1.29 us: per_device(): valid = (rows_here < jnp.sum(item_lengths)).astype(F32)[:, None]]
    ppermute x0 -> x35, waiting for transfers between devices: none -> 130 us  [swap(): lax.ppermute(array, axis, [(i, i ^ bit) for i in range(lax.axis_size(axis...]
    psum x2 -> x1, waiting for transfers between devices: 261 us -> 132 us  [per_device(): grad_qkv, grad_out_weight = lax.psum((grad_qkv, grad_out_weight), 'dp')]
    reduce_scatter x3 -> x0, waiting for transfers between devices: 102 us -> none  [the longest x2 57.7 us: own_rows(): lax.psum_scatter(partial_sum.astype(jnp.bfloat16), 'mp', scatter_dimensio...]
    psum x2 -> x0, blocking collectives: 62.7 us -> none  [the longest x1 40.1 us: per_device(): lax.psum((square_sums, grad_ln1_gain, grad_ln1_bias, grad_out_bias, grad_...]
    convert_element_type x17 -> x13, other arithmetic: 79.2 us -> 17.1 us  [the longest x8 9.05 us: add(): return (left.astype(F32) + right.astype(F32)).astype(left.dtype)]
  transfers between devices with their start and end apart: 8 -> 36, of which waited for: 7 -> 17; matrix products, arithmetic and copies ran while one was open for 11% -> 8% of each run, Pallas kernels for 0% -> 26%
where the time goes in v1:
time: 538 us; the launch traced here: 530 us
  waiting for transfers between devices  262 us (49%)
  Pallas kernels  151 us (28%)
  starting transfers between devices  41.2 us (8%)
  other arithmetic  28.6 us (5%)
  matrix products  16.4 us (3%)
  between operations  15.6 us (3%)
  local copies, waits for them, and re-layouts  15.4 us (3%)
    psum x1, waiting for transfers between devices, per_device(): grad_qkv, grad_out_weight = lax.psum((grad_qkv, grad_out_weight), 'dp')  132 us
    ppermute x35, waiting for transfers between devices, swap(): lax.ppermute(array, axis, [(i, i ^ bit) for i in range(lax.axis_size(axis...  130 us
    pallas_call x4, Pallas kernels, feed(): call(feed_body, (rows // tile,), [block, block, whole(w_up.shape), whole(...  41.7 us
    ppermute x35, starting transfers between devices, swap(): lax.ppermute(array, axis, [(i, i ^ bit) for i in range(lax.axis_size(axis...  41.1 us
    pallas_call x7, Pallas kernels, outer(): call(functools.partial(outer_body, count), (depth // tile,), [pl.BlockSpe...  35.6 us
    pallas_call x1, Pallas kernels, attend_back(): call(body, (1,), [scalars(), scalars()] + [whole((own_rows, width3))] * l...  29.2 us
    pallas_call x1, Pallas kernels, attend(): call(body, (1,), [scalars(), scalars()] + [whole((own_rows, width3))] * l...  18 us
    dot_general x8, matrix products, mxu(): return lax.dot_general(left, right, dims, preferred_element_type=F32)  16.4 us
  transfers between devices with their start and end apart: 36, of which 17 were waited for; matrix products, arithmetic and copies ran while one was open for 8% of the time, Pallas kernels for 26%

profile of v1, /device:TPU:0, one launch (start us, length us, event | category | flops | bytes accessed | tf_op | source)
XLA Modules:
  0.0 529.8 jit_solution(7269887252080711936)
XLA Ops:
  10.4 5.0 shard_map.271
  15.4 2.9 collective-permute-start.1
  21.0 21.6 %collective-permute-done.1.refs_6_ = bf16[512,1024]{1,0:T(8,128)(2,1)S(1)} collective-permute-done((bf16[512,1024]{1,0:T(8,128)(2,1)}, bf16[512,1024]{1,0:T(8,128)(2,1)S(1)}, u32[]{:S(2)}, u32[]{:S(2)}) %collective-permute-start.1) | collective-permute-done | bytes 1048608 | tf_op jit(solution)/shard_map/ppermute | solution.py:637
  43.2 3.1 add_convert_fusion.9.refs_0_
  46.3 6.6 %collective-permute-done.7.refs_6_.refs_2_ = bf16[256,1024]{1,0:T(8,128)(2,1)S(1)} collective-permute-done((bf16[256,1024]{1,0:T(8,128)(2,1)}, bf16[256,1024]{1,0:T(8,128)(2,1)S(1)}, u32[]{:S(2)}, u32[]{:S(2)}) %collective-permute-start.7) | collective-permute-done | bytes 524320 | tf_op jit(solution)/shard_map/ppermute | solution.py:637
  54.9 3.2 add_convert_fusion.8.refs_1_
  58.0 1.9 add_convert_fusion.6.refs_3_
  60.0 18.0 %shard_map.272 = (bf16[2048,256]{1,0:T(8,128)(2,1)}, f32[4,8,1,256]{3,2,1,0:T(1,128)}) custom-call(s32[5]{0:T(128)} %lengths.11, s32[1]{0:T(128)} %bitcast.place.place_ref, bf16[512,768]{1,0:T(8,128)(2,1)} %add_convert_fusion.9.refs_0_, bf16[512,768]{1,0:T(8,128)(2,1)} %add_convert_fusion.8.refs_1_, bf16[512,768]{1,0:T(8,128)(2,1)} %add_convert_fusion.7.refs_2_, ...), custom_call_target="tpu_custom_call" | custom-call | flops 2147483648 | bytes 5242880 | tf_op jit(solution)/shard_map/pallas_call | solution.py:265
  78.0 2.0 fusion.10
  84.3 4.3 collective-permute-done.5.refs_3_.refs_0_
  88.6 6.3 %collective-permute-done.4.refs_2_.refs_0_ = bf16[512,256]{1,0:T(8,128)(2,1)S(1)} collective-permute-done((bf16[512,256]{1,0:T(8,128)(2,1)S(1)}, bf16[512,256]{1,0:T(8,128)(2,1)S(1)}, u32[]{:S(2)}, u32[]{:S(2)}) %collective-permute-start.4) | collective-permute-done | bytes 262176 | tf_op jit(solution)/shard_map/ppermute | solution.py:637
  95.7 5.7 %shard_map.273 = (f32[512,1024]{1,0:T(8,128)}, bf16[512,1024]{1,0:T(8,128)(2,1)}, f32[1,1024]{1,0:T(1,128)}) custom-call(s32[5]{0:T(128)} %lengths.11, s32[1]{0:T(128)} %bitcast.place.place_ref, bf16[512,256]{1,0:T(8,128)(2,1)} %get-tuple-element.105.refs_0_, bf16[512,256]{1,0:T(8,128)(2,1)} %copy-done.16, bf16[512,256]{1,0:T(8,128)(2,1)} %copy-done.14, ...), custom_call_target="tpu_custom_call" | custom-call | flops 1073741824 | bytes 8388608 | tf_op jit(solution)/shard_map/pallas_call | solution.py:426
  103.2 14.2 %collective-permute-done.13.grad_mlp.refs_6_ = bf16[512,1024]{1,0:T(8,128)(2,1)S(1)} collective-permute-done((bf16[512,1024]{1,0:T(8,128)(2,1)S(1)}, bf16[512,1024]{1,0:T(8,128)(2,1)S(1)}, u32[]{:S(2)}, u32[]{:S(2)}) %collective-permute-start.13) | collective-permute-done | bytes 1048608 | tf_op jit(solution)/shard_map/ppermute | solution.py:637
  117.4 22.0 %collective-permute-done.12.normed.refs_2_ = bf16[512,1024]{1,0:T(8,128)(2,1)S(1)} collective-permute-done((bf16[512,1024]{1,0:T(8,128)(2,1)}, bf16[512,1024]{1,0:T(8,128)(2,1)S(1)}, u32[]{:S(2)}, u32[]{:S(2)}) %collective-permute-start.12) | collective-permute-done | bytes 1048608 | tf_op jit(solution)/shard_map/ppermute | solution.py:637
  139.9 3.6 collective-permute-done.14.normed.refs_3_
  144.4 10.5 %shard_map.277 = (bf16[512,1024]{1,0:T(8,128)(2,1)}, bf16[512,1024]{1,0:T(8,128)(2,1)}, bf16[512,1024]{1,0:T(8,128)(2,1)}, bf16[512,1024]{1,0:T(8,128)(2,1)}, f32[1,1024]{1,0:T(1,128)}) custom-call(bf16[512,1024]{1,0:T(8,128)(2,1)} %copy-done.30, bf16[512,1024]{1,0:T(8,128)(2,1)} %copy-done.32, bf16[1024,1024]{1,0:T(8,128)(2,1)} %w_up.7, ...), custom_call_target="tpu_custom_call" | custom-call | flops 4294967296 | bytes 10485760 | tf_op jit(solution)/shard_map/pallas_call | solution.py:482
  156.2 10.3 %shard_map.275 = (bf16[512,1024]{1,0:T(8,128)(2,1)}, bf16[512,1024]{1,0:T(8,128)(2,1)}, bf16[512,1024]{1,0:T(8,128)(2,1)}, bf16[512,1024]{1,0:T(8,128)(2,1)}, f32[1,1024]{1,0:T(1,128)}) custom-call(bf16[512,1024]{1,0:T(8,128)(2,1)} %copy-done.31, bf16[512,1024]{1,0:T(8,128)(2,1)} %collective-permute-done.10.grad_mlp.refs_5_, bf16[1024,1024]{1,0:T(8,128)(2,1)} %w_up.7, ...), custom_call_target="tpu_custom_call" | custom-call | flops 4294967296 | bytes 10485760 | tf_op jit(solution)/shard_map/pallas_call | solution.py:482
  166.9 10.3 %shard_map.276 = (bf16[512,1024]{1,0:T(8,128)(2,1)}, bf16[512,1024]{1,0:T(8,128)(2,1)}, bf16[512,1024]{1,0:T(8,128)(2,1)}, bf16[512,1024]{1,0:T(8,128)(2,1)}, f32[1,1024]{1,0:T(1,128)}) custom-call(bf16[512,1024]{1,0:T(8,128)(2,1)} %copy-done.28, bf16[512,1024]{1,0:T(8,128)(2,1)} %copy-done.29, bf16[1024,1024]{1,0:T(8,128)(2,1)} %w_up.7, ...), custom_call_target="tpu_custom_call" | custom-call | flops 4294967296 | bytes 10485760 | tf_op jit(solution)/shard_map/pallas_call | solution.py:482
  180.5 10.5 %shard_map.274 = (bf16[512,1024]{1,0:T(8,128)(2,1)}, bf16[512,1024]{1,0:T(8,128)(2,1)}, bf16[512,1024]{1,0:T(8,128)(2,1)}, bf16[512,1024]{1,0:T(8,128)(2,1)}, f32[1,1024]{1,0:T(1,128)}) custom-call(bf16[512,1024]{1,0:T(8,128)(2,1)} %get-tuple-element.56.normed.refs_0_, bf16[512,1024]{1,0:T(8,128)(2,1)} %copy-done.17, bf16[1024,1024]{1,0:T(8,128)(2,1)} %w_up.7, ...), custom_call_target="tpu_custom_call" | custom-call | flops 4294967296 | bytes 10485760 | tf_op jit(solution)/shard_map/pallas_call | solution.py:482
  191.1 2.6 add_convert_fusion.3.half_a
  193.7 8.7 %shard_map.288 = bf16[1024,1024]{1,0:T(8,128)(2,1)} custom-call(bf16[512,1024]{1,0:T(8,128)(2,1)} %get-tuple-element.87.refs_0_, bf16[512,1024]{1,0:T(8,128)(2,1)} %get-tuple-element.88.refs_1_, bf16[512,1024]{1,0:T(8,128)(2,1)} %get-tuple-element.89.refs_2_, bf16[512,1024]{1,0:T(8,128)(2,1)} %get-tuple-element.90.refs_3_, bf16[512,1024]{1,0:T(8,128)(2,1)} %copy-done.17, ...), custom_call_target="tpu_custom_call" | custom-call | flops 4294967296 | bytes 10485760 | tf_op jit(solution)/shard_map/pallas_call | solution.py:514
  205.1 6.7 %shard_map.279 = (f32[512,1024]{1,0:T(8,128)}, bf16[512,1024]{1,0:T(8,128)(2,1)}, bf16[512,256]{1,0:T(8,128)(2,1)}, bf16[512,256]{1,0:T(8,128)(2,1)}, bf16[512,2...) custom-call(s32[5]{0:T(128)} %lengths.11, s32[1]{0:T(128)} %bitcast.place.place_ref, ...), custom_call_target="tpu_custom_call" | custom-call | flops 1073741824 | bytes 12582912 | tf_op jit(solution)/shard_map/pallas_call | solution.py:558
  213.8 8.9 %shard_map.287 = bf16[1024,1024]{1,0:T(8,128)(2,1)} custom-call(bf16[512,1024]{1,0:T(8,128)(2,1)} %get-tuple-element.56.normed.refs_0_, bf16[512,1024]{1,0:T(8,128)(2,1)} %copy-done.31, bf16[512,1024]{1,0:T(8,128)(2,1)} %copy-done.28, bf16[512,1024]{1,0:T(8,128)(2,1)} %copy-done.30, bf16[512,1024]{1,0:T(8,128)(2,1)} %get-tuple-element.83.refs_4_, ...), custom_call_target="tpu_custom_call" | custom-call | flops 4294967296 | bytes 10485760 | tf_op jit(solution)/shard_map/pallas_call | solution.py:514
  222.7 2.6 shard_map.284
  225.6 2.6 shard_map.286
  228.4 2.6 shard_map.283
  230.9 2.6 shard_map.285
  234.4 29.2 %shard_map.280 = bf16[2048,768]{1,0:T(8,128)(2,1)} custom-call(s32[5]{0:T(128)} %lengths.11, s32[1]{0:T(128)} %bitcast.place.place_ref, bf16[512,768]{1,0:T(8,128)(2,1)} %add_convert_fusion.9.refs_0_, bf16[512,768]{1,0:T(8,128)(2,1)} %add_convert_fusion.8.refs_1_, bf16[512,768]{1,0:T(8,128)(2,1)} %add_convert_fusion.7.refs_2_, ...), custom_call_target="tpu_custom_call" | custom-call | flops 5368709120 | bytes 8388608 | tf_op jit(solution)/shard_map/pallas_call | solution.py:372
  265.5 3.6 fusion.9
  269.1 7.7 %shard_map.282 = bf16[768,1024]{1,0:T(8,128)(2,1)} custom-call(bf16[512,768]{1,0:T(8,128)(2,1)} %get-tuple-element.101.refs_0_, bf16[512,768]{1,0:T(8,128)(2,1)} %get-tuple-element.100.refs_1_, bf16[512,768]{1,0:T(8,128)(2,1)} %get-tuple-element.99.refs_2_, bf16[512,768]{1,0:T(8,128)(2,1)} %get-tuple-element.98.refs_3_, ...), custom_call_target="tpu_custom_call" | custom-call | flops 3221225472 | bytes 8912896 | tf_op jit(solution)/shard_map/pallas_call | solution.py:514
  280.3 2.3 convolution_convert_fusion
  285.3 2.0 convolution_convert_fusion.2
  291.4 18.2 %collective-permute-done.17.half_b = bf16[512,1024]{1,0:T(8,128)(2,1)S(1)} collective-permute-done((bf16[512,1024]{1,0:T(8,128)(2,1)S(1)}, bf16[512,1024]{1,0:T(8,128)(2,1)S(1)}, u32[]{:S(2)}, u32[]{:S(2)}) %collective-permute-start.17) | collective-permute-done | bytes 1048608 | tf_op jit(solution)/shard_map/ppermute | solution.py:637
  310.6 4.2 shard_map.278
  317.9 13.7 %collective-permute-done.26.half_b = bf16[512,1024]{1,0:T(8,128)(2,1)} collective-permute-done((bf16[512,1024]{1,0:T(8,128)(2,1)S(1)}, bf16[512,1024]{1,0:T(8,128)(2,1)}, u32[]{:S(2)}, u32[]{:S(2)}) %collective-permute-start.26) | collective-permute-done | bytes 1048608 | tf_op jit(solution)/shard_map/ppermute | solution.py:637
  331.7 4.8 shard_map.281
  340.8 2.1 collective-permute-done.28
  343.0 10.2 %collective-permute-start.29 = (f32[96,128]{1,0:T(8,128)S(1)}, f32[96,128]{1,0:T(8,128)S(1)}, u32[]{:S(2)}, u32[]{:S(2)}) collective-permute-start(f32[96,128]{1,0:T(8,128)S(1)} %fusion), channel_id=1, source_target_pairs={{0,4},{4,0},{8,12},{12,8},{16,20},{20,16},{24,28},{28,24},{1,5},{5... | collective-permute-start | bytes 147464 | tf_op jit(solution)/shard_map/ppermute | solution.py:637
  353.2 2.1 collective-permute-done.29
  355.3 6.9 %collective-permute-done.30 = f32[96,128]{1,0:T(8,128)S(1)} collective-permute-done((f32[96,128]{1,0:T(8,128)S(1)}, f32[96,128]{1,0:T(8,128)S(1)}, u32[]{:S(2)}, u32[]{:S(2)}) %collective-permute-start.30) | collective-permute-done | bytes 49184 | tf_op jit(solution)/shard_map/ppermute | solution.py:637
  362.2 9.3 %collective-permute-start.31 = (f32[96,128]{1,0:T(8,128)S(1)}, f32[96,128]{1,0:T(8,128)S(1)}, u32[]{:S(2)}, u32[]{:S(2)}) collective-permute-start(f32[96,128]{1,0:T(8,128)S(1)} %fusion.25), channel_id=1, source_target_pairs={{0,16},{4,20},{8,24},{12,28},{16,0},{20,4},{24,8},{28,12},{1,17},{... | collective-permute-start | bytes 147464 | tf_op jit(solution)/shard_map/ppermute | solution.py:637
  371.5 3.9 collective-permute-done.31
  377.8 2.5 fusion.2
  381.0 132.2 %all-reduce.4.cloned.1.call-done = (bf16[3,256,1024]{2,1,0:T(8,128)(2,1)}, bf16[256,1024]{1,0:T(8,128)(2,1)}, bf16[1024,1024]{1,0:T(8,128)(2,1)}, bf16[1024,1024]{1,0:T(8,128)(2,1)}) async-done(((bf16[3,256,1024]{2,1,0:T(8,128)(2,1)}, bf16[256,1024]{1,0:T(8,128)(2,1)}, bf16[1024,1024]{1,0:T(8,128)(2,1)}, bf16[1024,1024]{1,0:T(8,128)(2,1)}), (bf16[3,256,1024]{2,1,0:T(8,128)(2,1)}, ...) | async-done | bytes 6291472 | tf_op jit(solution)/shard_map/psum | solution.py:735
  513.1 2.2 convert_element_type.185
  515.4 2.1 reshape.102
  517.5 2.5 convert_element_type.186
  520.0 2.5 convert_element_type.187
  (166 shorter events, 50.8 us)
Async XLA Ops:
  7.2 36.0 %copy-start = (bf16[3,256,1024]{2,1,0:T(8,128)(2,1)S(1)}, bf16[3,256,1024]{2,1,0:T(8,128)(2,1)}, u32[]{:S(2)}) copy-start(bf16[3,256,1024]{2,1,0:T(8,128)(2,1)} %param.22) | copy-start | bytes 4718596
  7.2 505.9 %all-reduce.4.cloned.1.call-start = ((), (), s32[]{:S(2)}) async-start(), calls=%async_computation | async-start | bytes 12582912 | tf_op jit(solution)/shard_map/psum | solution.py:735
  15.4 27.1 %collective-permute-start.1 = (bf16[512,1024]{1,0:T(8,128)(2,1)}, bf16[512,1024]{1,0:T(8,128)(2,1)S(1)}, u32[]{:S(2)}, u32[]{:S(2)}) collective-permute-start(bf16[512,1024]{1,0:T(8,128)(2,1)} %get-tuple-element.53.refs_4_), channel_id=1, source_target_pairs={{0,2},{1,3},{2,0},{3,1},{4,6},{5,7},{6,4},{7,5},{8,10},{9,11},{10,... | collective-permute-start | bytes 3145736 | tf_op jit(solution)/shard_map/ppermute | solution.py:637
  18.4 34.6 %collective-permute-start.7 = (bf16[256,1024]{1,0:T(8,128)(2,1)}, bf16[256,1024]{1,0:T(8,128)(2,1)S(1)}, u32[]{:S(2)}, u32[]{:S(2)}) collective-permute-start(bf16[256,1024]{1,0:T(8,128)(2,1)} %refs_0_.1), channel_id=1, source_target_pairs={{0,2},{1,3},{2,0},{3,1},{4,6},{5,7},{6,4},{7,5},{8,10},{9,11},{10,... | collective-permute-start | bytes 1572872 | tf_op jit(solution)/shard_map/ppermute | solution.py:637
  18.4 64.0 %collective-permute-start.6 = (bf16[256,1024]{1,0:T(8,128)(2,1)}, bf16[256,1024]{1,0:T(8,128)(2,1)}, u32[]{:S(2)}, u32[]{:S(2)}) collective-permute-start(bf16[256,1024]{1,0:T(8,128)(2,1)} %refs_0_.1), channel_id=1, source_target_pairs={{0,1},{1,0},{2,3},{3,2},{4,5},{5,4},{6,7},{7,6},{8,9},{9,8},{10,11... | collective-permute-start | bytes 1572872 | tf_op jit(solution)/shard_map/ppermute | solution.py:637
  18.4 36.5 %collective-permute-start = (bf16[512,1024]{1,0:T(8,128)(2,1)}, bf16[512,1024]{1,0:T(8,128)(2,1)}, u32[]{:S(2)}, u32[]{:S(2)}) collective-permute-start(bf16[512,1024]{1,0:T(8,128)(2,1)} %get-tuple-element.53.refs_4_), channel_id=1, source_target_pairs={{0,1},{1,0},{2,3},{3,2},{4,5},{5,4},{6,7},{7,6},{8,9},{9,8},{10,11... | collective-permute-start | bytes 3145736 | tf_op jit(solution)/shard_map/ppermute | solution.py:637
  42.6 10.4 %copy-start.24 = (bf16[512,1024]{1,0:T(8,128)(2,1)}, bf16[512,1024]{1,0:T(8,128)(2,1)S(1)}, u32[]{:S(2)}) copy-start(bf16[512,1024]{1,0:T(8,128)(2,1)S(1)} %collective-permute-done.1.refs_6_) | copy-start | bytes 3145732
  42.6 15.5 %collective-permute-start.2 = (bf16[512,1024]{1,0:T(8,128)(2,1)S(1)}, bf16[512,1024]{1,0:T(8,128)(2,1)S(1)}, u32[]{:S(2)}, u32[]{:S(2)}) collective-permute-start(bf16[512,1024]{1,0:T(8,128)(2,1)S(1)} %collective-permute-done.1.refs_6_), channel_id=1, source_target_pairs={{0,1},{1,0},{2,3},{3,2},{4,5},{5,4},{6,7},{7,6},{8,9},{9,8},{10,11... | collective-permute-start | bytes 3145736 | tf_op jit(solution)/shard_map/ppermute | solution.py:637
  53.0 31.3 %collective-permute-start.8 = (bf16[256,1024]{1,0:T(8,128)(2,1)S(1)}, bf16[256,1024]{1,0:T(8,128)(2,1)S(1)}, u32[]{:S(2)}, u32[]{:S(2)}) collective-permute-start(bf16[256,1024]{1,0:T(8,128)(2,1)S(1)} %collective-permute-done.7.refs_6_.refs_2_), channel_id=1, source_target_pairs={{0,1},{1,0},{2,3},{3,2},{4,5},{5,4},{6,7},{7,6},{8,9},{9,8},{10,11... | collective-permute-start | bytes 1572872 | tf_op jit(solution)/shard_map/ppermute | solution.py:637
  80.0 8.5 %collective-permute-start.5 = (bf16[512,256]{1,0:T(8,128)(2,1)S(1)}, bf16[512,256]{1,0:T(8,128)(2,1)S(1)}, u32[]{:S(2)}, u32[]{:S(2)}) collective-permute-start(bf16[512,256]{1,0:T(8,128)(2,1)S(1)} %get-tuple-element.102), channel_id=1, source_target_pairs={{0,3},{1,2},{2,1},{3,0},{4,7},{5,6},{6,5},{7,4},{8,11},{9,10},{10,... | collective-permute-start | bytes 786440 | tf_op jit(solution)/shard_map/ppermute | solution.py:637
  81.9 13.0 %collective-permute-start.4 = (bf16[512,256]{1,0:T(8,128)(2,1)S(1)}, bf16[512,256]{1,0:T(8,128)(2,1)S(1)}, u32[]{:S(2)}, u32[]{:S(2)}) collective-permute-start(bf16[512,256]{1,0:T(8,128)(2,1)S(1)} %get-tuple-element.103), channel_id=1, source_target_pairs={{0,2},{1,3},{2,0},{3,1},{4,6},{5,7},{6,4},{7,5},{8,10},{9,11},{10,... | collective-permute-start | bytes 786440 | tf_op jit(solution)/shard_map/ppermute | solution.py:637
  82.2 12.7 %collective-permute-start.3 = (bf16[512,256]{1,0:T(8,128)(2,1)S(1)}, bf16[512,256]{1,0:T(8,128)(2,1)S(1)}, u32[]{:S(2)}, u32[]{:S(2)}) collective-permute-start(bf16[512,256]{1,0:T(8,128)(2,1)S(1)} %get-tuple-element.104), channel_id=1, source_target_pairs={{0,1},{1,0},{2,3},{3,2},{4,5},{5,4},{6,7},{7,6},{8,9},{9,8},{10,11... | collective-permute-start | bytes 786440 | tf_op jit(solution)/shard_map/ppermute | solution.py:637
  82.4 72.5 %copy-start.17 = (bf16[512,1024]{1,0:T(8,128)(2,1)}, bf16[512,1024]{1,0:T(8,128)(2,1)S(1)}, u32[]{:S(2)}) copy-start(bf16[512,1024]{1,0:T(8,128)(2,1)S(1)} %multiply_convert_fusion.grad_mlp.refs_4_) | copy-start | bytes 3145732
  82.5 34.9 %collective-permute-start.13 = (bf16[512,1024]{1,0:T(8,128)(2,1)S(1)}, bf16[512,1024]{1,0:T(8,128)(2,1)S(1)}, u32[]{:S(2)}, u32[]{:S(2)}) collective-permute-start(bf16[512,1024]{1,0:T(8,128)(2,1)S(1)} %multiply_convert_fusion.grad_mlp.refs_4_), channel_id=1, source_target_pairs={{0,2},{1,3},{2,0},{3,1},{4,6},{5,7},{6,4},{7,5},{8,10},{9,11},{10,... | collective-permute-start | bytes 3145736 | tf_op jit(solution)/shard_map/ppermute | solution.py:637
  84.3 10.6 %copy-start.6 = (bf16[256,1024]{1,0:T(8,128)(2,1)}, bf16[256,1024]{1,0:T(8,128)(2,1)S(1)}, u32[]{:S(2)}) copy-start(bf16[256,1024]{1,0:T(8,128)(2,1)S(1)} %collective-permute-done.8.refs_7_.refs_3_) | copy-start | bytes 1572868
  88.6 6.4 %copy-start.15 = (bf16[512,256]{1,0:T(8,128)(2,1)}, bf16[512,256]{1,0:T(8,128)(2,1)S(1)}, u32[]{:S(2)}) copy-start(bf16[512,256]{1,0:T(8,128)(2,1)S(1)} %collective-permute-done.5.refs_3_.refs_0_) | copy-start | bytes 786436
  101.4 38.0 %collective-permute-start.12 = (bf16[512,1024]{1,0:T(8,128)(2,1)}, bf16[512,1024]{1,0:T(8,128)(2,1)S(1)}, u32[]{:S(2)}, u32[]{:S(2)}) collective-permute-start(bf16[512,1024]{1,0:T(8,128)(2,1)} %get-tuple-element.56.normed.refs_0_), channel_id=1, source_target_pairs={{0,2},{1,3},{2,0},{3,1},{4,6},{5,7},{6,4},{7,5},{8,10},{9,11},{10,... | collective-permute-start | bytes 3145736 | tf_op jit(solution)/shard_map/ppermute | solution.py:637
  117.4 37.6 %copy-start.29 = (bf16[512,1024]{1,0:T(8,128)(2,1)}, bf16[512,1024]{1,0:T(8,128)(2,1)S(1)}, u32[]{:S(2)}) copy-start(bf16[512,1024]{1,0:T(8,128)(2,1)S(1)} %collective-permute-done.13.grad_mlp.refs_6_) | copy-start | bytes 3145732
  117.4 22.5 %collective-permute-start.15 = (bf16[512,1024]{1,0:T(8,128)(2,1)S(1)}, bf16[512,1024]{1,0:T(8,128)(2,1)S(1)}, u32[]{:S(2)}, u32[]{:S(2)}) collective-permute-start(bf16[512,1024]{1,0:T(8,128)(2,1)S(1)} %collective-permute-done.13.grad_mlp.refs_6_), channel_id=1, source_target_pairs={{0,1},{1,0},{2,3},{3,2},{4,5},{5,4},{6,7},{7,6},{8,9},{9,8},{10,11... | collective-permute-start | bytes 3145736 | tf_op jit(solution)/shard_map/ppermute | solution.py:637
  139.3 15.6 %copy-start.28 = (bf16[512,1024]{1,0:T(8,128)(2,1)}, bf16[512,1024]{1,0:T(8,128)(2,1)S(1)}, u32[]{:S(2)}) copy-start(bf16[512,1024]{1,0:T(8,128)(2,1)S(1)} %collective-permute-done.12.normed.refs_2_) | copy-start | bytes 3145732
  139.3 4.1 collective-permute-start.14
  139.3 15.8 %collective-permute-start.10 = (bf16[512,1024]{1,0:T(8,128)(2,1)S(1)}, bf16[512,1024]{1,0:T(8,128)(2,1)}, u32[]{:S(2)}, u32[]{:S(2)}) collective-permute-start(bf16[512,1024]{1,0:T(8,128)(2,1)S(1)} %multiply_convert_fusion.grad_mlp.refs_4_), channel_id=1, source_target_pairs={{0,1},{1,0},{2,3},{3,2},{4,5},{5,4},{6,7},{7,6},{8,9},{9,8},{10,11... | collective-permute-start | bytes 3145736 | tf_op jit(solution)/shard_map/ppermute | solution.py:637
  139.8 15.3 %collective-permute-start.9 = (bf16[512,1024]{1,0:T(8,128)(2,1)}, bf16[512,1024]{1,0:T(8,128)(2,1)S(1)}, u32[]{:S(2)}, u32[]{:S(2)}) collective-permute-start(bf16[512,1024]{1,0:T(8,128)(2,1)} %get-tuple-element.56.normed.refs_0_), channel_id=1, source_target_pairs={{0,1},{1,0},{2,3},{3,2},{4,5},{5,4},{6,7},{7,6},{8,9},{9,8},{10,11... | collective-permute-start | bytes 3145736 | tf_op jit(solution)/shard_map/ppermute | solution.py:637
  154.9 22.3 %collective-permute-start.19 = (bf16[512,1024]{1,0:T(8,128)(2,1)}, bf16[512,1024]{1,0:T(8,128)(2,1)S(1)}, u32[]{:S(2)}, u32[]{:S(2)}) collective-permute-start(bf16[512,1024]{1,0:T(8,128)(2,1)} %get-tuple-element.66), channel_id=1, source_target_pairs={{0,1},{1,0},{2,3},{3,2},{4,5},{5,4},{6,7},{7,6},{8,9},{9,8},{10,11... | collective-permute-start | bytes 3145736 | tf_op jit(solution)/shard_map/ppermute | solution.py:637
  166.5 24.6 %collective-permute-start.18 = (bf16[512,1024]{1,0:T(8,128)(2,1)}, bf16[512,1024]{1,0:T(8,128)(2,1)S(1)}, u32[]{:S(2)}, u32[]{:S(2)}) collective-permute-start(bf16[512,1024]{1,0:T(8,128)(2,1)} %get-tuple-element.64), channel_id=1, source_target_pairs={{0,1},{1,0},{2,3},{3,2},{4,5},{5,4},{6,7},{7,6},{8,9},{9,8},{10,11... | collective-permute-start | bytes 3145736 | tf_op jit(solution)/shard_map/ppermute | solution.py:637
  178.8 25.3 %collective-permute-start.20 = (bf16[512,1024]{1,0:T(8,128)(2,1)S(1)}, bf16[512,1024]{1,0:T(8,128)(2,1)S(1)}, u32[]{:S(2)}, u32[]{:S(2)}) collective-permute-start(bf16[512,1024]{1,0:T(8,128)(2,1)S(1)} %add_convert_fusion.2), channel_id=1, source_target_pairs={{0,2},{1,3},{2,0},{3,1},{4,6},{5,7},{6,4},{7,5},{8,10},{9,11},{10,... | collective-permute-start | bytes 3145736 | tf_op jit(solution)/shard_map/ppermute | solution.py:637
  211.9 21.7 %collective-permute-start.21 = (bf16[512,256]{1,0:T(8,128)(2,1)}, bf16[512,256]{1,0:T(8,128)(2,1)S(1)}, u32[]{:S(2)}, u32[]{:S(2)}) collective-permute-start(bf16[512,256]{1,0:T(8,128)(2,1)} %get-tuple-element.68), channel_id=1, source_target_pairs={{0,1},{1,0},{2,3},{3,2},{4,5},{5,4},{6,7},{7,6},{8,9},{9,8},{10,11... | collective-permute-start | bytes 786440 | tf_op jit(solution)/shard_map/ppermute | solution.py:637
  211.9 21.6 %collective-permute-start.22 = (bf16[512,256]{1,0:T(8,128)(2,1)}, bf16[512,256]{1,0:T(8,128)(2,1)S(1)}, u32[]{:S(2)}, u32[]{:S(2)}) collective-permute-start(bf16[512,256]{1,0:T(8,128)(2,1)} %get-tuple-element.69), channel_id=1, source_target_pairs={{0,2},{1,3},{2,0},{3,1},{4,6},{5,7},{6,4},{7,5},{8,10},{9,11},{10,... | collective-permute-start | bytes 786440 | tf_op jit(solution)/shard_map/ppermute | solution.py:637
  213.6 19.9 %collective-permute-start.23 = (bf16[512,256]{1,0:T(8,128)(2,1)}, bf16[512,256]{1,0:T(8,128)(2,1)S(1)}, u32[]{:S(2)}, u32[]{:S(2)}) collective-permute-start(bf16[512,256]{1,0:T(8,128)(2,1)} %get-tuple-element.70), channel_id=1, source_target_pairs={{0,3},{1,2},{2,1},{3,0},{4,7},{5,6},{6,5},{7,4},{8,11},{9,10},{10,... | collective-permute-start | bytes 786440 | tf_op jit(solution)/shard_map/ppermute | solution.py:637
  225.3 51.5 %collective-permute-start.32 = (bf16[256,1024]{1,0:T(8,128)(2,1)}, bf16[256,1024]{1,0:T(8,128)(2,1)S(1)}, u32[]{:S(2)}, u32[]{:S(2)}) collective-permute-start(bf16[256,1024]{1,0:T(8,128)(2,1)} %shard_map.284), channel_id=1, source_target_pairs={{0,1},{1,0},{2,3},{3,2},{4,5},{5,4},{6,7},{7,6},{8,9},{9,8},{10,11... | collective-permute-start | bytes 1572872 | tf_op jit(solution)/shard_map/ppermute | solution.py:637
  228.2 35.3 %collective-permute-start.33 = (bf16[256,1024]{1,0:T(8,128)(2,1)}, bf16[256,1024]{1,0:T(8,128)(2,1)S(1)}, u32[]{:S(2)}, u32[]{:S(2)}) collective-permute-start(bf16[256,1024]{1,0:T(8,128)(2,1)} %shard_map.286), channel_id=1, source_target_pairs={{0,1},{1,0},{2,3},{3,2},{4,5},{5,4},{6,7},{7,6},{8,9},{9,8},{10,11... | collective-permute-start | bytes 1572872 | tf_op jit(solution)/shard_map/ppermute | solution.py:637
  234.4 29.2 %copy-start.7 = (bf16[256,1024]{1,0:T(8,128)(2,1)S(1)}, bf16[256,1024]{1,0:T(8,128)(2,1)}, u32[]{:S(2)}) copy-start(bf16[256,1024]{1,0:T(8,128)(2,1)} %shard_map.285) | copy-start | bytes 1572868
  263.7 14.3 %collective-permute-start.34 = (bf16[256,1024]{1,0:T(8,128)(2,1)S(1)}, bf16[256,1024]{1,0:T(8,128)(2,1)S(1)}, u32[]{:S(2)}, u32[]{:S(2)}) collective-permute-start(bf16[256,1024]{1,0:T(8,128)(2,1)S(1)} %add_convert_fusion.11), channel_id=1, source_target_pairs={{0,2},{1,3},{2,0},{3,1},{4,6},{5,7},{6,4},{7,5},{8,10},{9,11},{10,... | collective-permute-start | bytes 1572872 | tf_op jit(solution)/shard_map/ppermute | solution.py:637
  269.1 8.9 %copy-start.8 = (bf16[256,1024]{1,0:T(8,128)(2,1)S(1)}, bf16[256,1024]{1,0:T(8,128)(2,1)}, u32[]{:S(2)}) copy-start(bf16[256,1024]{1,0:T(8,128)(2,1)} %shard_map.283) | copy-start | bytes 1572868
  280.3 2.9 collective-permute-start.16
  282.6 5.8 %collective-permute-start.25 = (bf16[512,1024]{1,0:T(8,128)(2,1)S(1)}, bf16[512,1024]{1,0:T(8,128)(2,1)S(1)}, u32[]{:S(2)}, u32[]{:S(2)}) collective-permute-start(bf16[512,1024]{1,0:T(8,128)(2,1)S(1)} %convolution_convert_fusion), channel_id=1, source_target_pairs={{0,1},{1,0},{2,3},{3,2},{4,5},{5,4},{6,7},{7,6},{8,9},{9,8},{10,11... | collective-permute-start | bytes 3145736 | tf_op jit(solution)/shard_map/ppermute | solution.py:637
  283.0 7.0 %collective-permute-start.11 = (bf16[512,1024]{1,0:T(8,128)(2,1)S(1)}, bf16[512,1024]{1,0:T(8,128)(2,1)S(1)}, u32[]{:S(2)}, u32[]{:S(2)}) collective-permute-start(bf16[512,1024]{1,0:T(8,128)(2,1)S(1)} %copy-done.26), channel_id=1, source_target_pairs={{0,1},{1,0},{2,3},{3,2},{4,5},{5,4},{6,7},{7,6},{8,9},{9,8},{10,11... | collective-permute-start | bytes 3145736 | tf_op jit(solution)/shard_map/ppermute | solution.py:637
  283.6 26.1 %collective-permute-start.17 = (bf16[512,1024]{1,0:T(8,128)(2,1)S(1)}, bf16[512,1024]{1,0:T(8,128)(2,1)S(1)}, u32[]{:S(2)}, u32[]{:S(2)}) collective-permute-start(bf16[512,1024]{1,0:T(8,128)(2,1)S(1)} %add_convert_fusion.4), channel_id=1, source_target_pairs={{0,2},{1,3},{2,0},{3,1},{4,6},{5,7},{6,4},{7,5},{8,10},{9,11},{10,... | collective-permute-start | bytes 3145736 | tf_op jit(solution)/shard_map/ppermute | solution.py:637
  287.3 29.2 %collective-permute-start.24 = (bf16[512,1024]{1,0:T(8,128)(2,1)}, bf16[512,1024]{1,0:T(8,128)(2,1)S(1)}, u32[]{:S(2)}, u32[]{:S(2)}) collective-permute-start(bf16[512,1024]{1,0:T(8,128)(2,1)} %convolution_convert_fusion.2), channel_id=1, source_target_pairs={{0,1},{1,0},{2,3},{3,2},{4,5},{5,4},{6,7},{7,6},{8,9},{9,8},{10,11... | collective-permute-start | bytes 3145736 | tf_op jit(solution)/shard_map/ppermute | solution.py:637
  288.8 42.8 %collective-permute-start.26 = (bf16[512,1024]{1,0:T(8,128)(2,1)S(1)}, bf16[512,1024]{1,0:T(8,128)(2,1)}, u32[]{:S(2)}, u32[]{:S(2)}) collective-permute-start(bf16[512,1024]{1,0:T(8,128)(2,1)S(1)} %add_convert_fusion), channel_id=1, source_target_pairs={{0,2},{1,3},{2,0},{3,1},{4,6},{5,7},{6,4},{7,5},{8,10},{9,11},{10,... | collective-permute-start | bytes 3145736 | tf_op jit(solution)/shard_map/ppermute | solution.py:637
  331.6 5.7 %copy-start.21 = (f32[1,1024]{1,0:T(1,128)S(1)}, f32[1,1024]{1,0:T(1,128)}, u32[]{:S(2)}) copy-start(f32[1,1024]{1,0:T(1,128)} %get-tuple-element.79) | copy-start | bytes 12292
  331.6 5.7 %copy-start.22 = (f32[1,1024]{1,0:T(1,128)S(1)}, f32[1,1024]{1,0:T(1,128)}, u32[]{:S(2)}) copy-start(f32[1,1024]{1,0:T(1,128)} %get-tuple-element.80) | copy-start | bytes 12292
  331.6 5.7 %copy-start.23 = (f32[1,1024]{1,0:T(1,128)S(1)}, f32[1,1024]{1,0:T(1,128)}, u32[]{:S(2)}) copy-start(f32[1,1024]{1,0:T(1,128)} %get-tuple-element.78) | copy-start | bytes 12292
  337.2 1.3 collective-permute-start.27
  338.6 4.3 collective-permute-start.28
  343.0 12.3 %collective-permute-start.29 = (f32[96,128]{1,0:T(8,128)S(1)}, f32[96,128]{1,0:T(8,128)S(1)}, u32[]{:S(2)}, u32[]{:S(2)}) collective-permute-start(f32[96,128]{1,0:T(8,128)S(1)} %fusion), channel_id=1, source_target_pairs={{0,4},{4,0},{8,12},{12,8},{16,20},{20,16},{24,28},{28,24},{1,5},{5... | collective-permute-start | bytes 147464 | tf_op jit(solution)/shard_map/ppermute | solution.py:637
  355.3 7.0 %collective-permute-start.30 = (f32[96,128]{1,0:T(8,128)S(1)}, f32[96,128]{1,0:T(8,128)S(1)}, u32[]{:S(2)}, u32[]{:S(2)}) collective-permute-start(f32[96,128]{1,0:T(8,128)S(1)} %fusion.3), channel_id=1, source_target_pairs={{0,8},{4,12},{8,0},{12,4},{16,24},{20,28},{24,16},{28,20},{1,9},{5... | collective-permute-start | bytes 147464 | tf_op jit(solution)/shard_map/ppermute | solution.py:637
  362.2 13.2 %collective-permute-start.31 = (f32[96,128]{1,0:T(8,128)S(1)}, f32[96,128]{1,0:T(8,128)S(1)}, u32[]{:S(2)}, u32[]{:S(2)}) collective-permute-start(f32[96,128]{1,0:T(8,128)S(1)} %fusion.25), channel_id=1, source_target_pairs={{0,16},{4,20},{8,24},{12,28},{16,0},{20,4},{24,8},{28,12},{1,17},{... | collective-permute-start | bytes 147464 | tf_op jit(solution)/shard_map/ppermute | solution.py:637
  (24 other events, 51.2 us)
Sparse Core Ops, SparseCore 0:
  279.2 233.8 all-reduce.3
